TPU v7x, 32 devices: a whole 2x2x4 slice. The times are simulated.
32 devices in a mesh: slab: 8 (over z, x), quad: 4 (over y, core).
Axes of the slice: x: 2, y: 2, z: 4, core: 2. Of those that a mesh axis runs over, the one named last changes fastest.
Arguments:
- right_side: float32 [32, 64, 1024], P('slab', 'quad'), may hold values from -16 to 16
- phase_label: int32 [32, 64, 1024], P('slab', 'quad'), may hold values 0 or 1
- density_gain: float32 [32, 64, 1024], P('slab', 'quad'), may hold values from 0.25 to 1.75
- subdomain: int32 [32, 64, 1024], P('slab', 'quad'), may hold values from 0 to 63, as said below
- block_factor: float32 [8, 256, 256], P('slab', 'quad'), may hold values from -0.03125 to 0.03125
- coupling: float32 [8, 256, 64], P('slab', 'quad'), may hold values from -0.75 to 0.75
Outputs:
- solution_field: float32 [32, 64, 1024], P('slab', 'quad')
- residual: float32 [32, 64, 1024], P('slab', 'quad')
Inputs may be any that keep to these rules, and one draw needn't show every extreme that they name: `subdomain`: within each device the subdomains are 8 x 8 contiguous tiles with jagged edges, each spanning the device's z-planes.
All inputs are finite; a program needn't handle non-finite values. No bound on the sum of `phase_label` on one device may be relied on, other than what follows from the above.
Results may differ from a plain program's by a relative error of at most 0.0075.
Values sent between devices are 32-bit elements; how exact they have to be, the bound alone decides.
A program may use at most 64 MiB of HBM per device.

v0:
```python
import jax
import jax.numpy as jnp
from jax import lax
from jax.sharding import PartitionSpec as P

LINE = 4
ITERS = 2


HIGH = lax.Precision.HIGHEST


def with_halo(value, sides, width):
    for axis, dim in sides:
        size, length = (lax.axis_size(axis), value.shape[dim])
        up = [(i, (i + 1) % size) for i in range(size - 1)]
        down = [(j, i) for i, j in up]
        last = lax.slice_in_dim(value, length - width, length, axis=dim)
        initial = lax.slice_in_dim(value, 0, width, axis=dim)
        before = lax.ppermute(last, axis, up)
        after = lax.ppermute(initial, axis, down)
        value = jnp.concatenate([before, value, after], axis=dim)
    return value


def prefix(value, axis, combine, identity, reverse):
    length, mine = (lax.axis_size(axis), lax.axis_index(axis))
    everything = jax.tree.map(lambda part: lax.all_gather(part, axis), value)
    start = jax.tree.map(
        lambda part, zero: jnp.broadcast_to(jnp.asarray(zero, part.dtype), part.shape),
        value,
        identity,
    )

    def turn(k, before):
        at = length - 1 - k if reverse else k
        reached = at > mine if reverse else at < mine
        new = combine(before, jax.tree.map(lambda part: part[at], everything))
        return jax.tree.map(lambda a, b: jnp.where(reached, a, b), new, before)

    return lax.fori_loop(0, length, turn, start)


def harmonic(here, there):
    return jnp.where(there > 0, 2.0 * here * there / (here + there), here)


def solve_along_line(diag, lower, upper, rhs):
    shape = rhs.shape
    dd = diag.reshape(-1, LINE, shape[1], shape[2])
    lo = lower.reshape(-1, LINE, shape[1], shape[2])
    up = upper.reshape(-1, LINE, shape[1], shape[2])
    rr = rhs.reshape(-1, LINE, shape[1], shape[2])
    gammas = []
    rhos = []
    denom = dd[:, 0]
    gammas.append(-up[:, 0] / denom)
    rhos.append(rr[:, 0] / denom)
    for j in range(1, LINE):
        denom = dd[:, j] + lo[:, j] * gammas[j - 1]
        gammas.append(-up[:, j] / denom)
        rhos.append((rr[:, j] + lo[:, j] * rhos[j - 1]) / denom)
    values = [None] * LINE
    values[LINE - 1] = rhos[LINE - 1]
    for j in range(LINE - 2, -1, -1):
        values[j] = rhos[j] - gammas[j] * values[j + 1]
    return jnp.stack(values, axis=1).reshape(shape)


def adjacent_cells(center, extended):
    xpad = jnp.pad(center, ((0, 0), (0, 0), (1, 1)))
    return (
        extended[:-2, 1:-1],
        extended[2:, 1:-1],
        extended[1:-1, :-2],
        extended[1:-1, 2:],
        xpad[:, :, :-2],
        xpad[:, :, 2:],
    )


def compose(earlier, later):
    return (
        jnp.dot(later[0], earlier[0], precision=HIGH),
        jnp.dot(later[0], earlier[1], precision=HIGH) + later[1],
    )


def restrict(subdomain, field, count):
    labels = lax.broadcasted_iota(jnp.int32, (count, 1), 0)

    def restrict_plane(total, pair):
        sub_plane, field_plane = pair
        onehot = (sub_plane.reshape(1, -1) == labels).astype(jnp.float32)
        return (total + jnp.dot(onehot, field_plane.reshape(-1), precision=HIGH), None)

    total, unused = lax.scan(restrict_plane, jnp.zeros((count,), jnp.float32), (subdomain, field))
    return total


def interpolate_coarse(subdomain, values):
    count = values.shape[0]
    labels = lax.broadcasted_iota(jnp.int32, (count, 1), 0)

    def interpolate_plane(sub_plane):
        onehot = (sub_plane.reshape(1, -1) == labels).astype(jnp.float32)
        return jnp.dot(values, onehot, precision=HIGH).reshape(sub_plane.shape)

    return lax.map(interpolate_plane, subdomain)


def body(right_side, phase_label, density_gain, subdomain, block_factor, coupling):
    mobility = 1.0 / (density_gain * (0.001 + 0.999 * phase_label.astype(jnp.float32)))
    mext = with_halo(mobility, (("slab", 0), ("quad", 1)), 1)
    near = adjacent_cells(mobility, mext)
    kz_lo = harmonic(mobility, near[0])
    kz_hi = harmonic(mobility, near[1])
    ky_lo = harmonic(mobility, near[2])
    ky_hi = harmonic(mobility, near[3])
    kx_lo = harmonic(mobility, near[4])
    kx_hi = harmonic(mobility, near[5])
    diag = kz_lo + kz_hi + ky_lo + ky_hi + kx_lo + kx_hi
    factor = block_factor[0]
    couple = coupling[0]
    count = couple.shape[0]

    def coarse_solve(coarse_rhs):
        eye = jnp.eye(count, dtype=jnp.float32)
        blank = jnp.zeros((count,), jnp.float32)
        before = prefix((couple, coarse_rhs), "slab", compose, (eye, blank), False)
        u_own = jnp.dot(couple, before[1], precision=HIGH) + coarse_rhs
        flipped = couple.T
        after = prefix(
            (flipped, jnp.dot(flipped, u_own, precision=HIGH)), "slab", compose, (eye, blank), True
        )
        w_own = u_own + after[1]
        return (u_own, w_own)

    def precondition(resid):
        block_part = solve_along_line(diag, kz_lo, kz_hi, resid)
        coarse_in = restrict(subdomain, resid, count)
        coarse_all = lax.all_gather(coarse_in, "quad", axis=0, tiled=True)
        coarse_rhs = jnp.dot(factor, coarse_all, precision=HIGH)
        u_own, w_own = coarse_solve(coarse_rhs)
        coarse_out = lax.psum_scatter(
            jnp.dot(factor.T, w_own, precision=HIGH), "quad", scatter_dimension=0, tiled=True
        )
        precond = block_part + interpolate_coarse(subdomain, coarse_out)
        rz_total = lax.psum(jnp.sum(resid * precond), ("slab", "quad"))
        return (precond, rz_total)

    solution_field = jnp.zeros_like(right_side)
    residual = right_side
    precond, rz = precondition(residual)
    search_direction = precond
    for step in range(ITERS):
        vector_with_halo = with_halo(search_direction, (("slab", 0), ("quad", 1)), 1)
        vector_neighbour = adjacent_cells(search_direction, vector_with_halo)
        image = (
            diag * search_direction
            - kz_lo * vector_neighbour[0]
            - kz_hi * vector_neighbour[1]
            - ky_lo * vector_neighbour[2]
            - ky_hi * vector_neighbour[3]
            - kx_lo * vector_neighbour[4]
            - kx_hi * vector_neighbour[5]
        )
        alpha = rz / lax.psum(jnp.sum(search_direction * image), ("slab", "quad"))
        solution_field = solution_field + alpha * search_direction
        residual = residual - alpha * image
        if step + 1 < ITERS:
            precond, residual_precond_next = precondition(residual)
            search_direction = precond + residual_precond_next / rz * search_direction
            rz = residual_precond_next
    return (solution_field, residual)


def solution(mesh):
    in_specs = (
        P("slab", "quad", None),
        P("slab", "quad", None),
        P("slab", "quad", None),
        P("slab", "quad", None),
        P("slab", "quad", None),
        P("slab", "quad", None),
    )
    out_specs = (P("slab", "quad", None), P("slab", "quad", None))
    return jax.shard_map(body, mesh=mesh, in_specs=in_specs, out_specs=out_specs, check_vma=False)
```

profile of v0, /device:TPU:0, one launch (start us, length us, event | category | flops | bytes accessed | tf_op | source)
XLA Modules:
  0.0 382.5 jit_solution(9030640740060971614)
XLA Ops:
  1.8 5.0 %collective-permute-start = (f32[1,16,1024]{2,1,0:T(8,128)S(1)}, f32[1,16,1024]{2,1,0:T(8,128)S(1)}, u32[]{:S(2)}, u32[]{:S(2)}) collective-permute-start(f32[1,16,1024]{2,1,0:T(8,128)S(1)} %get-tuple-element.803), channel_id=1, source_target_pairs={{0,4},{4,8},{8,12},{12,16},{16,20},{20,24},{24,28},{1,5},{5,9},{9,... | collective-permute-start | bytes 196616 | tf_op jit(solution)/shard_map/ppermute | solution.py:20
  8.1 33.1 %all_gather.42 = f32[8,64,64]{2,1,0:T(8,128)S(1)} all-gather(f32[1,64,64]{2,1,0:T(8,128)S(1)} %copy-done.3), channel_id=1, replica_groups=mesh['slab'=8,'quad'=4] {'slab'}, dimensions={0}, use_global_device_ids=true | all-gather | bytes 147456 | tf_op jit(solution)/shard_map/all_gather | solution.py:28
  41.4 9.0 %while.106 = (s32[]{:T(128)}, f32[64]{0:T(128)S(1)}, s32[4,16,1024]{2,1,0:T(8,128)S(1)}, f32[4,16,1024]{2,1,0:T(8,128)S(1)}, s32[]{:T(128)}, /*index=5*/s32[]{:T(128)}) while((s32[]{:T(128)}, f32[64]{0:T(128)S(1)}, s32[4,16,1024]{2,1,0:T(8,128)S(1)}, f32[4,16,1024]{2,1,0:T(8,128)S(1)}, s32[]{:T(128)}, /*index=5*/s32[]{:T(128)}) %tuple.251), condition=%wide.region_1.2_spmd.clone, body=%wide.region_0.1_spmd.clone.sunk | while | flops 13631619 | bytes 655959 | solution.py:97
  51.9 5.6 %all-reduce.3 = f32[256]{0:T(256)S(1)} all-reduce(f32[256]{0:T(256)S(1)} %dynamic-update-slice), channel_id=1, replica_groups=mesh['slab'=8,'quad'=4] {'quad'}, use_global_device_ids=true, to_apply=%add.3 | all-reduce | flops 256 | bytes 2048
  59.1 20.4 %all-reduce.4 = f32[512]{0:T(512)S(1)} all-reduce(f32[512]{0:T(512)S(1)} %dynamic-update-slice.1), channel_id=2, replica_groups=mesh['slab'=8,'quad'=4] {'slab'}, use_global_device_ids=true, to_apply=%add.4 | all-reduce | flops 512 | bytes 4096
  81.6 17.1 %all-reduce.5 = f32[512]{0:T(512)S(1)} all-reduce(f32[512]{0:T(512)S(1)} %dynamic-update-slice.2), channel_id=4, replica_groups=mesh['slab'=8,'quad'=4] {'slab'}, use_global_device_ids=true, to_apply=%add.5 | all-reduce | flops 512 | bytes 4096
  98.8 30.7 %all-gather.1 = f32[512,64]{1,0:T(8,128)S(1)} all-gather(f32[64,64]{1,0:T(8,128)S(1)} %bitcast.271), channel_id=3, replica_groups=mesh['slab'=8,'quad'=4] {'slab'}, dimensions={0}, use_global_device_ids=true | all-gather | bytes 147456 | tf_op jit(solution)/shard_map/all_gather | solution.py:28
  131.8 5.7 %all-reduce.9 = f32[256]{0:T(256)S(1)} all-reduce(f32[256]{0:T(256)S(1)} %bitcast.273), channel_id=7, replica_groups=mesh['slab'=8,'quad'=4] {'quad'}, use_global_device_ids=true, to_apply=%region_6.7.clone | all-reduce | flops 256 | bytes 2048
  140.9 5.9 %while.104 = (s32[]{:T(128)}, f32[4,16,1024]{2,1,0:T(8,128)S(1)}, s32[4,16,1024]{2,1,0:T(8,128)S(1)}, f32[64]{0:T(128)S(1)}, s32[]{:T(128)}) while((s32[]{:T(128)}, f32[4,16,1024]{2,1,0:T(8,128)S(1)}, s32[4,16,1024]{2,1,0:T(8,128)S(1)}, f32[64]{0:T(128)S(1)}, s32[]{:T(128)}) %tuple.248), condition=%wide.region_8.9_spmd.clone, body=%wide.region_7.8_spmd.clone.sunk | while | flops 13631490 | bytes 655685 | solution.py:109
  151.4 4.3 %collective-permute-done.5 = f32[1,16,1024]{2,1,0:T(8,128)S(1)} collective-permute-done((f32[1,16,1024]{2,1,0:T(8,128)S(1)}, f32[1,16,1024]{2,1,0:T(8,128)S(1)}, u32[]{:S(2)}, u32[]{:S(2)}) %collective-permute-start.5) | collective-permute-done | bytes 65568 | tf_op jit(solution)/shard_map/ppermute | solution.py:21
  156.3 3.4 collective-permute-start.6
  161.6 3.7 collective-permute-done.7
  167.5 41.8 %all-reduce.11 = (f32[]{:T(128)}, f32[]{:T(128)}) all-reduce(f32[]{:T(128)} %get-tuple-element.697, f32[]{:T(128)} %get-tuple-element.696), channel_id=1, replica_groups=mesh['slab'=8,'quad'=4] {'slab','quad'}, use_global_device_ids=true, to_apply=%region_10.11 | all-reduce | flops 2 | bytes 16 | tf_op jit(solution)/shard_map/psum | solution.py:149
  210.6 9.0 %while.109 = (s32[]{:T(128)}, f32[64]{0:T(128)S(1)}, s32[4,16,1024]{2,1,0:T(8,128)S(1)}, f32[4,16,1024]{2,1,0:T(8,128)S(1)}, s32[]{:T(128)}, /*index=5*/s32[]{:T(128)}) while((s32[]{:T(128)}, f32[64]{0:T(128)S(1)}, s32[4,16,1024]{2,1,0:T(8,128)S(1)}, f32[4,16,1024]{2,1,0:T(8,128)S(1)}, s32[]{:T(128)}, ...), condition=%wide.region_14.15_spmd.clone, body=%wide.region_13.14_spmd.clone.sunk | while | flops 13631619 | bytes 655959 | solution.py:97
  219.8 6.0 %all-reduce.6 = f32[256]{0:T(256)S(1)} all-reduce(f32[256]{0:T(256)S(1)} %dynamic-update-slice.3), channel_id=1, replica_groups=mesh['slab'=8,'quad'=4] {'quad'}, use_global_device_ids=true, to_apply=%add.6 | all-reduce | flops 256 | bytes 2048
  226.2 20.8 %all-reduce.7 = f32[512]{0:T(512)S(1)} all-reduce(f32[512]{0:T(512)S(1)} %dynamic-update-slice.4), channel_id=5, replica_groups=mesh['slab'=8,'quad'=4] {'slab'}, use_global_device_ids=true, to_apply=%add.7 | all-reduce | flops 512 | bytes 4096
  249.1 17.1 %all-reduce.8 = f32[512]{0:T(512)S(1)} all-reduce(f32[512]{0:T(512)S(1)} %dynamic-update-slice.5), channel_id=6, replica_groups=mesh['slab'=8,'quad'=4] {'slab'}, use_global_device_ids=true, to_apply=%add.8 | all-reduce | flops 512 | bytes 4096
  267.9 6.0 %all-reduce.10 = f32[256]{0:T(256)S(1)} all-reduce(f32[256]{0:T(256)S(1)} %bitcast.274), channel_id=8, replica_groups=mesh['slab'=8,'quad'=4] {'quad'}, use_global_device_ids=true, to_apply=%region_19.20.clone | all-reduce | flops 256 | bytes 2048
  274.1 5.9 %while.105 = (s32[]{:T(128)}, f32[4,16,1024]{2,1,0:T(8,128)S(1)}, s32[4,16,1024]{2,1,0:T(8,128)S(1)}, f32[64]{0:T(128)S(1)}, s32[]{:T(128)}) while((s32[]{:T(128)}, f32[4,16,1024]{2,1,0:T(8,128)S(1)}, s32[4,16,1024]{2,1,0:T(8,128)S(1)}, f32[64]{0:T(128)S(1)}, s32[]{:T(128)}) %tuple.250), condition=%wide.region_21.22_spmd.clone, body=%wide.region_20.21_spmd.clone.sunk | while | flops 13631490 | bytes 655685 | solution.py:109
  280.8 37.1 %psum.30 = f32[]{:T(128)} all-reduce(f32[]{:T(128)} %multiply_reduce_fusion.1), channel_id=1, replica_groups=mesh['slab'=8,'quad'=4] {'slab','quad'}, use_global_device_ids=true, to_apply=%region_23.24 | all-reduce | flops 1 | bytes 8 | tf_op jit(solution)/shard_map/psum | solution.py:149
  319.3 4.3 %collective-permute-start.8 = (f32[1,16,1024]{2,1,0:T(8,128)S(1)}, f32[1,16,1024]{2,1,0:T(8,128)S(1)}, u32[]{:S(2)}, u32[]{:S(2)}) collective-permute-start(f32[1,16,1024]{2,1,0:T(8,128)S(1)} %get-tuple-element.799), channel_id=1, source_target_pairs={{0,4},{4,8},{8,12},{12,16},{16,20},{20,24},{24,28},{1,5},{5,9},{9,... | collective-permute-start | bytes 196616 | tf_op jit(solution)/shard_map/ppermute | solution.py:20
  325.5 4.3 %collective-permute-done.9 = f32[1,16,1024]{2,1,0:T(8,128)S(1)} collective-permute-done((f32[1,16,1024]{2,1,0:T(8,128)S(1)}, f32[1,16,1024]{2,1,0:T(8,128)S(1)}, u32[]{:S(2)}, u32[]{:S(2)}) %collective-permute-start.9) | collective-permute-done | bytes 65568 | tf_op jit(solution)/shard_map/ppermute | solution.py:21
  332.5 4.5 %collective-permute-done.11 = f32[6,1,1024]{2,1,0:T(1,128)S(1)} collective-permute-done((f32[6,1,1024]{2,1,0:T(1,128)S(1)}, f32[6,1,1024]{2,1,0:T(1,128)S(1)}, u32[]{:S(2)}, u32[]{:S(2)}) %collective-permute-start.11) | collective-permute-done | bytes 24608 | tf_op jit(solution)/shard_map/ppermute | solution.py:21
  338.3 42.0 %psum.31 = f32[]{:T(128)} all-reduce(f32[]{:T(128)} %get-tuple-element.772), channel_id=1, replica_groups=mesh['slab'=8,'quad'=4] {'slab','quad'}, use_global_device_ids=true, to_apply=%region_25.26 | all-reduce | flops 1 | bytes 8 | tf_op jit(solution)/shard_map/psum | solution.py:168
  (249 shorter events, 67.6 us)
Async XLA Ops:
  0.6 58.1 %copy-start = (f32[1,64,256]{2,1,0:T(8,128)S(1)}, f32[1,64,256]{2,1,0:T(8,128)}, u32[]{:S(2)}) copy-start(f32[1,64,256]{2,1,0:T(8,128)} %param.26) | copy-start | bytes 196612
  0.6 7.5 %copy-start.3 = (f32[1,64,64]{2,1,0:T(8,128)S(1)}, f32[1,64,64]{2,1,0:T(8,128)}, u32[]{:S(2)}) copy-start(f32[1,64,64]{2,1,0:T(8,128)} %param.27) | copy-start | bytes 49156
  1.8 39.6 %copy-start.1 = (s32[4,16,1024]{2,1,0:T(8,128)S(1)}, s32[4,16,1024]{2,1,0:T(8,128)}, u32[]{:S(2)}) copy-start(s32[4,16,1024]{2,1,0:T(8,128)} %param.25) | copy-start | bytes 786436
  1.8 39.6 %copy-start.2 = (f32[4,16,1024]{2,1,0:T(8,128)S(1)}, f32[4,16,1024]{2,1,0:T(8,128)}, u32[]{:S(2)}) copy-start(f32[4,16,1024]{2,1,0:T(8,128)} %param.22) | copy-start | bytes 786436
  1.8 135.8 %collective-permute-start = (f32[1,16,1024]{2,1,0:T(8,128)S(1)}, f32[1,16,1024]{2,1,0:T(8,128)S(1)}, u32[]{:S(2)}, u32[]{:S(2)}) collective-permute-start(f32[1,16,1024]{2,1,0:T(8,128)S(1)} %get-tuple-element.803), channel_id=1, source_target_pairs={{0,4},{4,8},{8,12},{12,16},{16,20},{20,24},{24,28},{1,5},{5,9},{9,... | collective-permute-start | bytes 196616 | tf_op jit(solution)/shard_map/ppermute | solution.py:20
  6.8 130.8 %collective-permute-start.1 = (f32[1,16,1024]{2,1,0:T(8,128)S(1)}, f32[1,16,1024]{2,1,0:T(8,128)S(1)}, u32[]{:S(2)}, u32[]{:S(2)}) collective-permute-start(f32[1,16,1024]{2,1,0:T(8,128)S(1)} %get-tuple-element.804), channel_id=1, source_target_pairs={{4,0},{8,4},{12,8},{16,12},{20,16},{24,20},{28,24},{5,1},{9,5},{13... | collective-permute-start | bytes 196616 | tf_op jit(solution)/shard_map/ppermute | solution.py:21
  41.4 9.0 %copy-start.12 = (u32[32]{0:T(128)S(1)}, u32[32]{0:T(128)}, u32[]{:S(2)}) copy-start(u32[32]{0:T(128)} %constant.194) | copy-start | bytes 388
  41.4 16.1 %copy-start.13 = (u32[32]{0:T(128)S(1)}, u32[32]{0:T(128)}, u32[]{:S(2)}) copy-start(u32[32]{0:T(128)} %constant.199) | copy-start | bytes 388
  137.6 9.1 %collective-permute-start.2 = (f32[6,1,1024]{2,1,0:T(1,128)S(1)}, f32[6,1,1024]{2,1,0:T(1,128)S(1)}, u32[]{:S(2)}, u32[]{:S(2)}) collective-permute-start(f32[6,1,1024]{2,1,0:T(1,128)S(1)} %get-tuple-element.795), channel_id=1, source_target_pairs={{0,1},{1,2},{2,3},{4,5},{5,6},{6,7},{8,9},{9,10},{10,11},{12,13},{... | collective-permute-start | bytes 73736 | tf_op jit(solution)/shard_map/ppermute | solution.py:20
  139.5 7.3 %collective-permute-start.3 = (f32[6,1,1024]{2,1,0:T(1,128)S(1)}, f32[6,1,1024]{2,1,0:T(1,128)S(1)}, u32[]{:S(2)}, u32[]{:S(2)}) collective-permute-start(f32[6,1,1024]{2,1,0:T(1,128)S(1)} %get-tuple-element.794), channel_id=1, source_target_pairs={{1,0},{2,1},{3,2},{5,4},{6,5},{7,6},{9,8},{10,9},{11,10},{13,12},{... | collective-permute-start | bytes 73736 | tf_op jit(solution)/shard_map/ppermute | solution.py:21
  146.8 0.6 copy-start.7
  148.2 3.2 collective-permute-start.4
  149.5 6.2 %collective-permute-start.5 = (f32[1,16,1024]{2,1,0:T(8,128)S(1)}, f32[1,16,1024]{2,1,0:T(8,128)S(1)}, u32[]{:S(2)}, u32[]{:S(2)}) collective-permute-start(f32[1,16,1024]{2,1,0:T(8,128)S(1)} %get-tuple-element.802), channel_id=1, source_target_pairs={{4,0},{8,4},{12,8},{16,12},{20,16},{24,20},{28,24},{5,1},{9,5},{13... | collective-permute-start | bytes 196616 | tf_op jit(solution)/shard_map/ppermute | solution.py:21
  151.4 4.3 %copy-start.4 = (f32[1,16,1024]{2,1,0:T(8,128)}, f32[1,16,1024]{2,1,0:T(8,128)S(1)}, u32[]{:S(2)}) copy-start(f32[1,16,1024]{2,1,0:T(8,128)S(1)} %collective-permute-done.4) | copy-start | bytes 196612
  155.7 0.6 copy-start.5
  156.3 4.7 %collective-permute-start.6 = (f32[6,1,1024]{2,1,0:T(1,128)S(1)}, f32[6,1,1024]{2,1,0:T(1,128)S(1)}, u32[]{:S(2)}, u32[]{:S(2)}) collective-permute-start(f32[6,1,1024]{2,1,0:T(1,128)S(1)} %get-tuple-element.792), channel_id=1, source_target_pairs={{0,1},{1,2},{2,3},{4,5},{5,6},{6,7},{8,9},{9,10},{10,11},{12,13},{... | collective-permute-start | bytes 73736 | tf_op jit(solution)/shard_map/ppermute | solution.py:20
  159.7 5.6 %collective-permute-start.7 = (f32[6,1,1024]{2,1,0:T(1,128)S(1)}, f32[6,1,1024]{2,1,0:T(1,128)}, u32[]{:S(2)}, u32[]{:S(2)}) collective-permute-start(f32[6,1,1024]{2,1,0:T(1,128)S(1)} %get-tuple-element.793), channel_id=1, source_target_pairs={{1,0},{2,1},{3,2},{5,4},{6,5},{7,6},{9,8},{10,9},{11,10},{13,12},{... | collective-permute-start | bytes 73736 | tf_op jit(solution)/shard_map/ppermute | solution.py:21
  274.1 5.9 %copy-start.6 = (f32[1,1,16,1024]{3,2,1,0:T(8,128)S(1)}, f32[1,1,16,1024]{3,2,1,0:T(8,128)}, u32[]{:S(2)}) copy-start(f32[1,1,16,1024]{3,2,1,0:T(8,128)} %get-tuple-element.785) | copy-start | bytes 196612
  319.3 17.7 %copy-start.8 = (f32[6,1,1024]{2,1,0:T(1,128)S(1)}, f32[6,1,1024]{2,1,0:T(1,128)}, u32[]{:S(2)}) copy-start(f32[6,1,1024]{2,1,0:T(1,128)} %copy-done.7) | copy-start | bytes 73732
  319.3 17.7 %copy-start.10 = (f32[6,1,1024]{2,1,0:T(1,128)S(1)}, f32[6,1,1024]{2,1,0:T(1,128)}, u32[]{:S(2)}) copy-start(f32[6,1,1024]{2,1,0:T(1,128)} %copy-done.9) | copy-start | bytes 73732
  319.3 6.2 %collective-permute-start.8 = (f32[1,16,1024]{2,1,0:T(8,128)S(1)}, f32[1,16,1024]{2,1,0:T(8,128)S(1)}, u32[]{:S(2)}, u32[]{:S(2)}) collective-permute-start(f32[1,16,1024]{2,1,0:T(8,128)S(1)} %get-tuple-element.799), channel_id=1, source_target_pairs={{0,4},{4,8},{8,12},{12,16},{16,20},{20,24},{24,28},{1,5},{5,9},{9,... | collective-permute-start | bytes 196616 | tf_op jit(solution)/shard_map/ppermute | solution.py:20
  323.6 6.2 %collective-permute-start.9 = (f32[1,16,1024]{2,1,0:T(8,128)S(1)}, f32[1,16,1024]{2,1,0:T(8,128)S(1)}, u32[]{:S(2)}, u32[]{:S(2)}) collective-permute-start(f32[1,16,1024]{2,1,0:T(8,128)S(1)} %get-tuple-element.800), channel_id=1, source_target_pairs={{4,0},{8,4},{12,8},{16,12},{20,16},{24,20},{28,24},{5,1},{9,5},{13... | collective-permute-start | bytes 196616 | tf_op jit(solution)/shard_map/ppermute | solution.py:21
  329.9 2.6 collective-permute-start.10
  331.2 5.8 %collective-permute-start.11 = (f32[6,1,1024]{2,1,0:T(1,128)S(1)}, f32[6,1,1024]{2,1,0:T(1,128)S(1)}, u32[]{:S(2)}, u32[]{:S(2)}) collective-permute-start(f32[6,1,1024]{2,1,0:T(1,128)S(1)} %get-tuple-element.791), channel_id=1, source_target_pairs={{1,0},{2,1},{3,2},{5,4},{6,5},{7,6},{9,8},{10,9},{11,10},{13,12},{... | collective-permute-start | bytes 73736 | tf_op jit(solution)/shard_map/ppermute | solution.py:21
  (2 other events, 1.2 us)
where the time goes:
time: 384 us; the launch traced here: 383 us
  blocking collectives  283 us (74%)
  matrix products  34.5 us (9%)
  starting transfers between devices  24.9 us (6%)
  waiting for transfers between devices  17.9 us (5%)
  other arithmetic  7.76 us (2%)
  between operations  7.04 us (2%)
  local copies, waits for them, and re-layouts  6.07 us (2%)
    unnamed x8, blocking collectives  98.8 us
    psum x2, blocking collectives, precondition(): rz_total = lax.psum(jnp.sum(resid * precond), ('slab', 'quad'))  78.9 us
    all_gather x2, blocking collectives, prefix(): everything = jax.tree.map(lambda part: lax.all_gather(part, axis), value)  63.9 us
    psum x1, blocking collectives, body(): alpha = rz / lax.psum(jnp.sum(search_direction * image), ('slab', 'quad'))  42 us
    ppermute x6, starting transfers between devices, with_halo(): before = lax.ppermute(last, axis, up)  17.1 us
    ppermute x6, waiting for transfers between devices, with_halo(): after = lax.ppermute(initial, axis, down)  16.7 us
    dot_general x8, matrix products, restrict_plane(): jnp.dot(onehot, field_plane.reshape(-1), precision=HIGH)  16.6 us
    dot_general x8, matrix products, interpolate_plane(): return jnp.dot(values, onehot, precision=HIGH).reshape(sub_plane.shape)  11 us
  transfers between devices with their start and end apart: 12, of which 6 were waited for; matrix products, arithmetic and copies ran while one was open for 5% of the time, Pallas kernels for 0%

commit v1 on v0

v1 whole, which is shorter than its diff:
```python
import functools

import jax
import jax.numpy as jnp
from jax import lax
from jax.experimental import pallas as pl
from jax.experimental.pallas import tpu as pltpu
from jax.sharding import PartitionSpec as P

LINE = 4
ITERS = 2
MESH = pl.DeviceIdType.MESH
F32 = jnp.float32
BF16 = jnp.bfloat16


def kernel(ns, nq, b_ref, phase_ref, gain_ref, sub_ref, fac_ref, cpl_ref, x_ref, r_ref,
           kz, kyl, kyh, kxl, kxh, diag, inv, gam, hot_hi, hot_lo, p0, q0, bj, zz,
           cg, qbuf, sbuf, rbuf, dbuf, ebuf, fbuf, zhalo, yhalo, ysend,
           cg_ss, cg_rs, q_ss, q_rs, s_ss, s_rs, r_ss, r_rs, d_ss, d_rs, e_ss, e_rs, f_ss, f_rs, h_ss, h_rs):
    k = lax.axis_index("slab")
    q = lax.axis_index("quad")
    cz, cy, nx = b_ref.shape
    count = cpl_ref.shape[2]
    pending = []

    barrier = pltpu.get_barrier_semaphore()
    for d in range(1, ns):
        pl.semaphore_signal(barrier, inc=1, device_id={"slab": lax.rem(k + d, ns)}, device_id_type=MESH)
    for d in range(1, nq):
        pl.semaphore_signal(barrier, inc=1, device_id={"quad": lax.rem(q + d, nq)}, device_id_type=MESH)

    def copies(axis, me, n, buf, ss, rs):
        out = []
        for d in range(1, n):
            out.append(pltpu.make_async_remote_copy(
                src_ref=buf.at[me], dst_ref=buf.at[me], send_sem=ss.at[d], recv_sem=rs.at[d],
                device_id={axis: lax.rem(me + d, n)}, device_id_type=MESH))
        return out

    def gather_start(axis, me, n, buf, ss, rs):
        for c in copies(axis, me, n, buf, ss, rs):
            c.start()
            pending.append(c)

    def gather_wait(axis, me, n, buf, ss, rs):
        for d in range(1, n):
            at = lax.rem(me + n - d, n)
            pltpu.make_async_remote_copy(
                src_ref=buf.at[at], dst_ref=buf.at[at], send_sem=ss.at[d], recv_sem=rs.at[d],
                device_id={axis: at}, device_id_type=MESH).wait_recv()

    row = lax.broadcasted_iota(jnp.int32, (cy, nx), 0)
    lane = lax.broadcasted_iota(jnp.int32, (cy, nx), 1)
    sub8 = lax.broadcasted_iota(jnp.int32, (8, 128), 0)
    lane8 = lax.broadcasted_iota(jnp.int32, (8, 128), 1)
    eye = (lax.broadcasted_iota(jnp.int32, (count, count), 0)
           == lax.broadcasted_iota(jnp.int32, (count, count), 1)).astype(F32)

    def halo_parts(slot, src):
        up, down = jnp.minimum(k + 1, ns - 1), jnp.maximum(k - 1, 0)
        right, left = jnp.minimum(q + 1, nq - 1), jnp.maximum(q - 1, 0)

        def copy(s, dst, i, axis, to):
            return pltpu.make_async_remote_copy(
                src_ref=s, dst_ref=dst, send_sem=h_ss.at[slot, i], recv_sem=h_rs.at[slot, i],
                device_id={axis: to}, device_id_type=MESH)

        return (
            (k < ns - 1, k > 0, copy(src.at[cz - 1], zhalo.at[slot, 0], 0, "slab", up)),
            (k > 0, k < ns - 1, copy(src.at[0], zhalo.at[slot, 1], 1, "slab", down)),
            (q < nq - 1, q > 0, copy(ysend.at[slot, 1], yhalo.at[slot, 0], 2, "quad", right)),
            (q > 0, q < nq - 1, copy(ysend.at[slot, 0], yhalo.at[slot, 1], 3, "quad", left)),
        )

    def halo_clear(slot):
        for buf, i, edge in ((zhalo, 0, k == 0), (zhalo, 1, k == ns - 1),
                             (yhalo, 0, q == 0), (yhalo, 1, q == nq - 1)):
            @pl.when(edge)
            def _(buf=buf, i=i):
                buf[slot, i] = jnp.zeros(buf.shape[2:], F32)

    def halo_start(slot, src):
        for j in range(cz):
            ysend[slot, 0, j:j + 1] = src[j, 0:1]
            ysend[slot, 1, j:j + 1] = src[j, cy - 1:cy]
        for sends, unused, c in halo_parts(slot, src):
            @pl.when(sends)
            def _(c=c):
                c.start()

    def halo_wait(slot, src):
        for sends, receives, c in halo_parts(slot, src):
            @pl.when(receives)
            def _(c=c):
                c.wait_recv()

            @pl.when(sends)
            def _(c=c):
                c.wait_send()

    def y_below(slot, plane, j):
        return jnp.where(row == 0, yhalo[slot, 0, j:j + 1], pltpu.roll(plane, 1, 0))

    def y_above(slot, plane, j):
        return jnp.where(row == cy - 1, yhalo[slot, 1, j:j + 1], pltpu.roll(plane, cy - 1, 0))

    def harmonic(here, there):
        return jnp.where(there > 0, 2.0 * here * there / (here + there), here)

    def restrict(planes):
        total = None
        for j in range(cz):
            high = planes[j].astype(BF16)
            low = (planes[j] - high.astype(F32)).astype(BF16)
            lhs = jnp.concatenate([part * hot_hi[j, h] for part in (high, low) for h in range(8)], axis=0)
            now = lax.dot_general(lhs, hot_lo[j], (((1,), (1,)), ((), ())), preferred_element_type=F32)
            total = now if total is None else total + now
        total = total[:8 * cy] + total[8 * cy:]
        spot = lax.broadcasted_iota(jnp.int32, total.shape, 0) % cy
        across = lax.broadcasted_iota(jnp.int32, total.shape, 1) // 8
        total = jnp.where(spot == across, total, 0.0)
        tile = jnp.concatenate(
            [jnp.sum(total[cy * h:cy * (h + 1)], axis=0, keepdims=True) for h in range(8)], axis=0)
        for shift in (8, 16, 32, 64):
            tile = tile + pltpu.roll(tile, shift, 1)
        return jnp.sum(jnp.where(sub8 == lane8 // 8, tile, 0.0), axis=0, keepdims=True)

    def partial(left, right):
        total = left[0] * right[0]
        for j in range(1, cz):
            total = total + left[j] * right[j]
        total = total[:8] + total[8:]
        tile = total[:, :128]
        for c in range(1, nx // 128):
            tile = tile + total[:, 128 * c:128 * (c + 1)]
        return jnp.sum(tile, axis=0, keepdims=True)

    def solve_lines(planes):
        rho = [planes[0] * inv[0]]
        for j in range(1, LINE):
            rho.append((planes[j] + kz[j] * rho[j - 1]) * inv[j])
        values = [None] * LINE
        values[LINE - 1] = rho[LINE - 1]
        for j in range(LINE - 2, -1, -1):
            values[j] = rho[j] - gam[j] * values[j + 1]
        return values

    def message(first, second):
        return jnp.where(sub8 == 0, first, second)

    def coarse_rhs(slot):
        rows = [qbuf[slot, i, 0:1] for i in range(nq)]
        pieces = [rows[2 * i] + pltpu.roll(rows[2 * i + 1], 64, 1) for i in range(nq // 2)]
        whole = jnp.concatenate(pieces, axis=1)
        column = jnp.sum(fac_ref[0] * whole, axis=1, keepdims=True)
        return jnp.sum(jnp.concatenate([eye, jnp.zeros_like(eye)], axis=1) * column, axis=0, keepdims=True)

    def chain(rhs):
        us = [rhs[0][:, :count]]
        sq_row, sq_col = us[0] * us[0], None
        for i in range(1, ns):
            if i % 2:
                now = jnp.sum(cg[i] * us[i - 1] + eye * rhs[i][:, :count], axis=1, keepdims=True)
                sq_col = now * now if sq_col is None else sq_col + now * now
            else:
                now = jnp.sum(cg[i] * us[i - 1], axis=0, keepdims=True) + rhs[i][:, :count]
                sq_row = sq_row + now * now
            us.append(now)
        w = us[ns - 1]
        own_row = jnp.zeros((1, count), F32)
        own_col = jnp.where(k == ns - 1, w, 0.0)
        for i in range(ns - 1, 0, -1):
            if i % 2:
                w = jnp.sum(cg[i] * w, axis=0, keepdims=True) + us[i - 1]
                own_row = jnp.where(k == i - 1, w, own_row)
            else:
                w = jnp.sum(cg[i] * w, axis=1, keepdims=True) + us[i - 1]
                own_col = jnp.where(k == i - 1, w, own_col)
        own = own_col + jnp.sum(eye * own_row, axis=1, keepdims=True)
        square = jnp.sum(sq_row, axis=1, keepdims=True) + jnp.sum(sq_col, axis=0, keepdims=True)
        share = jnp.sum(fac_ref[0] * own, axis=0, keepdims=True)
        return share, square

    def interpolate(table, j):
        wide = jnp.broadcast_to(table, (cy, 128))
        return jnp.concatenate(
            [jnp.take_along_axis(wide, sub_ref[j, :, 128 * c:128 * (c + 1)], axis=1, mode="promise_in_bounds")
             for c in range(nx // 128)], axis=1)

    def own_table(slot):
        total = rbuf[slot, 0]
        for i in range(1, nq):
            total = total + rbuf[slot, i]
        table = total[0:1, :128]
        for i in range(1, nq // 2):
            table = jnp.where(q // 2 == i, total[0:1, 128 * i:128 * (i + 1)], table)
        table = jnp.where(q % 2 == 1, pltpu.roll(table, 64, 1), table)
        return table, total

    def tile_sum(buf, n):
        total = buf[0]
        for i in range(1, n):
            total = total + buf[i]
        return total

    def apply(slot, planes):
        images = []
        for j in range(cz):
            below = planes[j - 1] if j > 0 else zhalo[slot, 0]
            above = planes[j + 1] if j < cz - 1 else zhalo[slot, 1]
            v = planes[j]
            images.append(
                diag[j] * v - kz[j] * below - kz[j + 1] * above
                - kyl[j] * y_below(slot, v, j) - kyh[j] * y_above(slot, v, j)
                - kxl[j] * pltpu.roll(v, 1, 1) - kxh[j] * pltpu.roll(v, nx - 1, 1))
        return images

    couple = cpl_ref[0]
    cg[k] = jnp.where(k % 2 == 1, couple, couple.T)
    for j in range(cz):
        zz[j] = 1.0 / (gain_ref[j] * (0.001 + 0.999 * phase_ref[j].astype(F32)))
    for slot in range(3):
        halo_clear(slot)
    pl.semaphore_wait(barrier, ns - 1 + nq - 1)
    halo_start(0, zz)
    gather_start("slab", k, ns, cg, cg_ss, cg_rs)

    for j in range(cz):
        label = sub_ref[j]
        high, low = label // 8, label % 8
        for h in range(8):
            hot_hi[j, h] = jnp.where(high == h, 1.0, 0.0).astype(BF16)
        digit = lax.broadcasted_iota(jnp.int32, (8, nx), 0)
        hot_lo[j] = jnp.concatenate(
            [jnp.where(low[y:y + 1] == digit, 1.0, 0.0) for y in range(cy)], axis=0).astype(BF16)

    right_side = [b_ref[j] for j in range(cz)]
    first_in = restrict(right_side)

    m = [zz[j] for j in range(cz)]
    kx_lo = []
    for j in range(cz):
        lo = jnp.where(lane == 0, m[j], harmonic(m[j], pltpu.roll(m[j], 1, 1)))
        hi = jnp.where(lane == nx - 1, m[j], pltpu.roll(lo, nx - 1, 1))
        kx_lo.append(lo + hi)
        kxl[j] = jnp.where(lane == 0, 0.0, lo)
        kxh[j] = jnp.where(lane == nx - 1, 0.0, hi)
    halo_wait(0, zz)
    kz[0] = harmonic(m[0], zhalo[0, 0])
    for j in range(1, cz):
        kz[j] = harmonic(m[j - 1], m[j])
    kz[cz] = harmonic(m[cz - 1], zhalo[0, 1])
    for j in range(cz):
        lo = harmonic(m[j], y_below(0, m[j], j))
        last = harmonic(m[j][cy - 1:cy], yhalo[0, 1, j:j + 1])
        hi = jnp.where(row == cy - 1, last, pltpu.roll(lo, cy - 1, 0))
        kyl[j] = lo
        kyh[j] = hi
        diag[j] = kz[j] + kz[j + 1] + lo + hi + kx_lo[j]
    previous = None
    for j in range(LINE):
        denom = diag[j] if j == 0 else diag[j] + kz[j] * previous
        inverse = 1.0 / denom
        inv[j] = inverse
        if j < LINE - 1:
            previous = -kz[j + 1] * inverse
            gam[j] = previous

    block = solve_lines(right_side)
    for j in range(cz):
        bj[j] = block[j]
    qbuf[0, q] = message(first_in, partial(right_side, block))
    gather_start("quad", q, nq, qbuf.at[0], q_ss.at[0], q_rs.at[0])
    gather_wait("quad", q, nq, qbuf.at[0], q_ss.at[0], q_rs.at[0])
    sbuf[0, k] = message(coarse_rhs(0), tile_sum(qbuf.at[0], nq)[1:2])
    gather_start("slab", k, ns, sbuf.at[0], s_ss.at[0], s_rs.at[0])
    gather_wait("slab", k, ns, cg, cg_ss, cg_rs)
    gather_wait("slab", k, ns, sbuf.at[0], s_ss.at[0], s_rs.at[0])
    rhs_first = [sbuf[0, i, 0:1] for i in range(ns)]
    share, square = chain(rhs_first)
    sub_wide = lax.broadcasted_iota(jnp.int32, (8, nq * count), 0)
    rbuf[0, q] = jnp.where(sub_wide == 0, share, square)
    gather_start("quad", q, nq, rbuf.at[0], r_ss.at[0], r_rs.at[0])
    rz_block = jnp.sum(tile_sum(sbuf.at[0], ns)[1:2], axis=1, keepdims=True)
    gather_wait("quad", q, nq, rbuf.at[0], r_ss.at[0], r_rs.at[0])
    table, total = own_table(0)
    rz = rz_block + total[1:2, 0:1]
    for j in range(cz):
        p0[j] = bj[j] + interpolate(table, j)
    halo_start(1, p0)
    halo_wait(1, p0)
    direction = [p0[j] for j in range(cz)]
    image = apply(1, direction)
    for j in range(cz):
        q0[j] = image[j]

    qbuf[1, q] = message(restrict(image), partial(direction, image))
    gather_start("quad", q, nq, qbuf.at[1], q_ss.at[1], q_rs.at[1])
    image_block = solve_lines([q0[j] for j in range(cz)])
    for j in range(cz):
        zz[j] = image_block[j]
    gather_wait("quad", q, nq, qbuf.at[1], q_ss.at[1], q_rs.at[1])
    sbuf[1, k] = message(coarse_rhs(1), tile_sum(qbuf.at[1], nq)[1:2])
    gather_start("slab", k, ns, sbuf.at[1], s_ss.at[1], s_rs.at[1])
    gather_wait("slab", k, ns, sbuf.at[1], s_ss.at[1], s_rs.at[1])
    alpha = rz / jnp.sum(tile_sum(sbuf.at[1], ns)[1:2], axis=1, keepdims=True)
    share, square = chain([sbuf[0, i, 0:1] - alpha * sbuf[1, i, 0:1] for i in range(ns)])
    resid = [b_ref[j] - alpha * q0[j] for j in range(cz)]
    block = [bj[j] - alpha * zz[j] for j in range(cz)]
    for j in range(cz):
        r_ref[j] = resid[j]
        bj[j] = block[j]
    dots = jnp.concatenate([partial(resid, block)] + [jnp.zeros((1, 128), F32)] * (nq * count // 128 - 1), axis=1)
    rbuf[1, q] = jnp.where(sub_wide == 0, share, jnp.where(sub_wide == 1, square, dots))
    gather_start("quad", q, nq, rbuf.at[1], r_ss.at[1], r_rs.at[1])
    gather_wait("quad", q, nq, rbuf.at[1], r_ss.at[1], r_rs.at[1])
    table, total = own_table(1)
    dbuf[k] = jnp.broadcast_to(total[2:3, :128], (8, 128))
    gather_start("slab", k, ns, dbuf, d_ss, d_rs)
    for j in range(cz):
        zz[j] = bj[j] + interpolate(table, j)
    halo_start(2, zz)
    halo_wait(2, zz)
    image = apply(2, [zz[j] for j in range(cz)])
    gather_wait("slab", k, ns, dbuf, d_ss, d_rs)
    rz_next = total[1:2, 0:1] + jnp.sum(tile_sum(dbuf, ns)[0:1], axis=1, keepdims=True)
    beta = rz_next / rz
    direction = [zz[j] + beta * p0[j] for j in range(cz)]
    image = [image[j] + beta * q0[j] for j in range(cz)]
    ebuf[q] = jnp.broadcast_to(partial(direction, image), (8, 128))
    gather_start("quad", q, nq, ebuf, e_ss, e_rs)
    for j in range(cz):
        zz[j] = direction[j]
        q0[j] = image[j]
        x_ref[j] = alpha * p0[j]
    gather_wait("quad", q, nq, ebuf, e_ss, e_rs)
    fbuf[k] = tile_sum(ebuf, nq)
    gather_start("slab", k, ns, fbuf, f_ss, f_rs)
    gather_wait("slab", k, ns, fbuf, f_ss, f_rs)
    last = rz_next / jnp.sum(tile_sum(fbuf, ns)[0:1], axis=1, keepdims=True)
    for j in range(cz):
        x_ref[j] = x_ref[j] + last * zz[j]
        r_ref[j] = r_ref[j] - last * q0[j]
    for c in pending:
        c.wait_send()


def solution(mesh):
    ns, nq = mesh.shape["slab"], mesh.shape["quad"]

    def body(right_side, phase_label, density_gain, subdomain, block_factor, coupling):
        cz, cy, nx = right_side.shape
        count = coupling.shape[2]
        field = pltpu.VMEM((cz, cy, nx), F32)
        dma = pltpu.SemaphoreType.DMA
        shape = jax.ShapeDtypeStruct((cz, cy, nx), F32)
        return tuple(pl.pallas_call(
            functools.partial(kernel, ns, nq),
            out_shape=(shape, shape),
            in_specs=[pl.BlockSpec(memory_space=pltpu.VMEM)] * 6,
            out_specs=(pl.BlockSpec(memory_space=pltpu.VMEM),) * 2,
            scratch_shapes=[
                pltpu.VMEM((cz + 1, cy, nx), F32), field, field, field, field, field, field, field,
                pltpu.VMEM((cz, 8, cy, nx), BF16), pltpu.VMEM((cz, 8 * cy, nx), BF16),
                field, field, field, field,
                pltpu.VMEM((ns, count, count), F32),
                pltpu.VMEM((2, nq, 8, 128), F32), pltpu.VMEM((2, ns, 8, 128), F32),
                pltpu.VMEM((2, nq, 8, nq * count), F32), pltpu.VMEM((ns, 8, 128), F32),
                pltpu.VMEM((nq, 8, 128), F32), pltpu.VMEM((ns, 8, 128), F32),
                pltpu.VMEM((3, 2, cy, nx), F32), pltpu.VMEM((3, 2, cz, nx), F32), pltpu.VMEM((3, 2, cz, nx), F32),
                dma((ns,)), dma((ns,)), dma((2, nq)), dma((2, nq)), dma((2, ns)), dma((2, ns)),
                dma((2, nq)), dma((2, nq)), dma((ns,)), dma((ns,)), dma((nq,)), dma((nq,)),
                dma((ns,)), dma((ns,)), dma((3, 4)), dma((3, 4)),
            ],
            compiler_params=pltpu.CompilerParams(
                collective_id=0, has_side_effects=True, vmem_limit_bytes=40 * 1024 * 1024),
        )(right_side, phase_label, density_gain, subdomain, block_factor, coupling))

    spec = P("slab", "quad", None)
    return jax.shard_map(body, mesh=mesh, in_specs=(spec,) * 6, out_specs=(spec, spec), check_vma=False)
```

time: 384 us -> 60.3 us (0.16)
  blocking collectives: 283 us -> 0 us
  Pallas kernels: 0 us -> 52.5 us
  matrix products: 34.5 us -> 0 us
  starting transfers between devices: 24.9 us -> 0 us
  waiting for transfers between devices: 17.9 us -> 0 us
  other arithmetic: 7.76 us -> 0 us
  between operations: 7.04 us -> 0.65 us
    psum x3 -> x0, blocking collectives: 121 us -> none  [the longest x2 78.9 us: precondition(): rz_total = lax.psum(jnp.sum(resid * precond), ('slab', 'quad'))]
    unnamed x8 -> x0, blocking collectives: 98.8 us -> none
    all_gather x2 -> x0, blocking collectives: 63.9 us -> none  [prefix(): everything = jax.tree.map(lambda part: lax.all_gather(part, axis), value)]
    pallas_call x0 -> x1, Pallas kernels: none -> 52.5 us  [body(): pl.pallas_call(functools.partial(kernel, ns, nq), out_shape=(shape, shape...]
    dot_general x56 -> x0, matrix products: 34.5 us -> none  [the longest x8 16.6 us: restrict_plane(): jnp.dot(onehot, field_plane.reshape(-1), precision=HIGH)]
    ppermute x12 -> x0, starting transfers between devices: 24.9 us -> none  [the longest x6 17.1 us: with_halo(): before = lax.ppermute(last, axis, up)]
    ppermute x12 -> x0, waiting for transfers between devices: 17.9 us -> none  [the longest x6 16.7 us: with_halo(): after = lax.ppermute(initial, axis, down)]
    reduce_sum x3 -> x0, other arithmetic: 4.22 us -> none  [the longest x2 3.55 us: body(): alpha = rz / lax.psum(jnp.sum(search_direction * image), ('slab', 'quad'))]
  transfers between devices with their start and end apart: 12 -> 0, of which waited for: 6 -> 0; matrix products, arithmetic and copies ran while one was open for 5% -> 0% of each run, Pallas kernels for 0% -> 0%
where the time goes in v1:
time: 60.3 us; the launch traced here: 60 us
  Pallas kernels  52.5 us (87%)
  local copies, waits for them, and re-layouts  6.8 us (11%)
  between operations  0.65 us (1%)
    pallas_call x1, Pallas kernels, body(): pl.pallas_call(functools.partial(kernel, ns, nq), out_shape=(shape, shape...  52.5 us
    unnamed x14, local copies, waits for them, and re-layouts  6.8 us

profile of v1, /device:TPU:0, one launch (start us, length us, event | category | flops | bytes accessed | tf_op | source)
XLA Modules:
  0.0 60.0 jit_solution(13420889980470387238)
XLA Ops:
  0.6 0.0 copy-start
  0.6 0.9 %copy-done = f32[4,16,1024]{2,1,0:T(8,128)S(1)} copy-done((f32[4,16,1024]{2,1,0:T(8,128)S(1)}, f32[4,16,1024]{2,1,0:T(8,128)}, u32[]{:S(2)}) %copy-start) | copy-done | bytes 262168
  1.6 0.0 copy-start.1
  1.6 0.9 %copy-done.1 = s32[4,16,1024]{2,1,0:T(8,128)S(1)} copy-done((s32[4,16,1024]{2,1,0:T(8,128)S(1)}, s32[4,16,1024]{2,1,0:T(8,128)}, u32[]{:S(2)}) %copy-start.1) | copy-done | bytes 262168
  2.5 0.0 copy-start.2
  2.5 0.9 %copy-done.2 = f32[4,16,1024]{2,1,0:T(8,128)S(1)} copy-done((f32[4,16,1024]{2,1,0:T(8,128)S(1)}, f32[4,16,1024]{2,1,0:T(8,128)}, u32[]{:S(2)}) %copy-start.2) | copy-done | bytes 262168
  3.5 0.0 copy-start.3
  3.5 0.9 %copy-done.3 = s32[4,16,1024]{2,1,0:T(8,128)S(1)} copy-done((s32[4,16,1024]{2,1,0:T(8,128)S(1)}, s32[4,16,1024]{2,1,0:T(8,128)}, u32[]{:S(2)}) %copy-start.3) | copy-done | bytes 262168
  4.4 0.0 copy-start.4
  4.4 0.8 %copy-done.4 = f32[1,64,256]{2,1,0:T(8,128)S(1)} copy-done((f32[1,64,256]{2,1,0:T(8,128)S(1)}, f32[1,64,256]{2,1,0:T(8,128)}, u32[]{:S(2)}) %copy-start.4) | copy-done | bytes 65560
  5.3 0.0 copy-start.5
  5.3 0.8 %copy-done.5 = f32[1,64,64]{2,1,0:T(8,128)S(1)} copy-done((f32[1,64,64]{2,1,0:T(8,128)S(1)}, f32[1,64,64]{2,1,0:T(8,128)}, u32[]{:S(2)}) %copy-start.5) | copy-done | bytes 16408
  6.0 52.5 %shard_map.77 = (f32[4,16,1024]{2,1,0:T(8,128)S(1)}, f32[4,16,1024]{2,1,0:T(8,128)S(1)}) custom-call(f32[4,16,1024]{2,1,0:T(8,128)S(1)} %copy-done, s32[4,16,1024]{2,1,0:T(8,128)S(1)} %copy-done.1, f32[4,16,1024]{2,1,0:T(8,128)S(1)} %copy-done.2, s32[4,16,1024]{2,1,0:T(8,128)S(1)} %copy-done.3, f32[1,64,256]{2,1,0:T(8,128)S(1)} %copy-done.4, ...), custom_call_target="tpu_custom_call" | custom-call | tf_op jit(solution)/shard_map/pallas_call | solution.py:358
  58.5 0.7 %copy.10 = f32[4,16,1024]{2,1,0:T(8,128)} copy(f32[4,16,1024]{2,1,0:T(8,128)S(1)} %get-tuple-element.4) | data formatting | bytes 524288
  59.3 0.7 %copy.11 = f32[4,16,1024]{2,1,0:T(8,128)} copy(f32[4,16,1024]{2,1,0:T(8,128)S(1)} %get-tuple-element.5) | data formatting | bytes 524288
Async XLA Ops:
  0.6 1.0 %copy-start = (f32[4,16,1024]{2,1,0:T(8,128)S(1)}, f32[4,16,1024]{2,1,0:T(8,128)}, u32[]{:S(2)}) copy-start(f32[4,16,1024]{2,1,0:T(8,128)} %b_ref.1) | copy-start | bytes 786436
  1.6 0.9 %copy-start.1 = (s32[4,16,1024]{2,1,0:T(8,128)S(1)}, s32[4,16,1024]{2,1,0:T(8,128)}, u32[]{:S(2)}) copy-start(s32[4,16,1024]{2,1,0:T(8,128)} %phase_ref.1) | copy-start | bytes 786436
  2.5 0.9 %copy-start.2 = (f32[4,16,1024]{2,1,0:T(8,128)S(1)}, f32[4,16,1024]{2,1,0:T(8,128)}, u32[]{:S(2)}) copy-start(f32[4,16,1024]{2,1,0:T(8,128)} %gain_ref.1) | copy-start | bytes 786436
  3.5 0.9 %copy-start.3 = (s32[4,16,1024]{2,1,0:T(8,128)S(1)}, s32[4,16,1024]{2,1,0:T(8,128)}, u32[]{:S(2)}) copy-start(s32[4,16,1024]{2,1,0:T(8,128)} %sub_ref.1) | copy-start | bytes 786436
  4.4 0.8 %copy-start.4 = (f32[1,64,256]{2,1,0:T(8,128)S(1)}, f32[1,64,256]{2,1,0:T(8,128)}, u32[]{:S(2)}) copy-start(f32[1,64,256]{2,1,0:T(8,128)} %fac_ref.1) | copy-start | bytes 196612
  5.3 0.8 %copy-start.5 = (f32[1,64,64]{2,1,0:T(8,128)S(1)}, f32[1,64,64]{2,1,0:T(8,128)}, u32[]{:S(2)}) copy-start(f32[1,64,64]{2,1,0:T(8,128)} %cpl_ref.1) | copy-start | bytes 49156

commit v2 on v1

--- a/solution.py
+++ b/solution.py
@@ -14,15 +14,20 @@
 BF16 = jnp.bfloat16
 
 
-def kernel(ns, nq, b_ref, phase_ref, gain_ref, sub_ref, fac_ref, cpl_ref, x_ref, r_ref,
-           kz, kyl, kyh, kxl, kxh, diag, inv, gam, hot_hi, hot_lo, p0, q0, bj, zz,
-           cg, qbuf, sbuf, rbuf, dbuf, ebuf, fbuf, zhalo, yhalo, ysend,
-           cg_ss, cg_rs, q_ss, q_rs, s_ss, s_rs, r_ss, r_rs, d_ss, d_rs, e_ss, e_rs, f_ss, f_rs, h_ss, h_rs):
+def kernel(ns, nq, b_hbm, phase_hbm, gain_hbm, sub_hbm, fac_hbm, cpl_hbm, x_out, p_out, r_out, q_out, step_ref,
+           b_ref, phase_ref, gain_ref, sub_ref, fac_ref, cpl_ref, x_ref, r_ref, in_sem, out_sem, kz, kyl, kyh, kxl, kxh, diag, inv, gam, hot_hi, hot_lo, p0, q0, bj, zz,
+           cg, cgw, qbuf, sbuf, rbuf, ebuf, fbuf, zhalo, yhalo, ysend,
+           cg_ss, cg_rs, q_ss, q_rs, s_ss, s_rs, r_ss, r_rs, e_ss, e_rs, f_ss, f_rs, h_ss, h_rs):
     k = lax.axis_index("slab")
     q = lax.axis_index("quad")
     cz, cy, nx = b_ref.shape
     count = cpl_ref.shape[2]
     pending = []
+    loads = [pltpu.make_async_copy(src, dst, in_sem.at[i]) for i, (src, dst) in enumerate((
+        (phase_hbm, phase_ref), (gain_hbm, gain_ref), (cpl_hbm, cpl_ref),
+        (sub_hbm, sub_ref), (b_hbm, b_ref), (fac_hbm, fac_ref)))]
+    for c in loads:
+        c.start()
 
     barrier = pltpu.get_barrier_semaphore()
     for d in range(1, ns):
@@ -216,19 +221,25 @@
                 - kxl[j] * pltpu.roll(v, 1, 1) - kxh[j] * pltpu.roll(v, nx - 1, 1))
         return images
 
-    couple = cpl_ref[0]
-    cg[k] = jnp.where(k % 2 == 1, couple, couple.T)
-    for j in range(cz):
-        zz[j] = 1.0 / (gain_ref[j] * (0.001 + 0.999 * phase_ref[j].astype(F32)))
     for slot in range(3):
         halo_clear(slot)
+    loads[0].wait()
+    loads[1].wait()
+    for j in range(cz):
+        zz[j] = 1.0 / (gain_ref[j] * (0.001 + 0.999 * phase_ref[j].astype(F32)))
     pl.semaphore_wait(barrier, ns - 1 + nq - 1)
     halo_start(0, zz)
-    gather_start("slab", k, ns, cg, cg_ss, cg_rs)
-
+    loads[2].wait()
+    couple = cpl_ref[0]
+    couple = jnp.where(k % 2 == 1, couple, couple.T)
+    cgw[k] = jnp.concatenate([couple[:count // 2], couple[count // 2:]], axis=1)
+    gather_start("slab", k, ns, cgw, cg_ss, cg_rs)
+
+    loads[3].wait()
+    loads[4].wait()
     for j in range(cz):
         label = sub_ref[j]
-        high, low = label // 8, label % 8
+        high, low = label >> 3, label & 7
         for h in range(8):
             hot_hi[j, h] = jnp.where(high == h, 1.0, 0.0).astype(BF16)
         digit = lax.broadcasted_iota(jnp.int32, (8, nx), 0)
@@ -236,7 +247,8 @@
             [jnp.where(low[y:y + 1] == digit, 1.0, 0.0) for y in range(cy)], axis=0).astype(BF16)
 
     right_side = [b_ref[j] for j in range(cz)]
-    first_in = restrict(right_side)
+    qbuf[0, q] = jnp.broadcast_to(restrict(right_side), (8, 128))
+    gather_start("quad", q, nq, qbuf.at[0], q_ss.at[0], q_rs.at[0])
 
     m = [zz[j] for j in range(cz)]
     kx_lo = []
@@ -270,22 +282,25 @@
     block = solve_lines(right_side)
     for j in range(cz):
         bj[j] = block[j]
-    qbuf[0, q] = message(first_in, partial(right_side, block))
-    gather_start("quad", q, nq, qbuf.at[0], q_ss.at[0], q_rs.at[0])
+    own_dot = partial(right_side, block)
+    loads[5].wait()
     gather_wait("quad", q, nq, qbuf.at[0], q_ss.at[0], q_rs.at[0])
-    sbuf[0, k] = message(coarse_rhs(0), tile_sum(qbuf.at[0], nq)[1:2])
+    sbuf[0, k] = message(coarse_rhs(0), own_dot)
     gather_start("slab", k, ns, sbuf.at[0], s_ss.at[0], s_rs.at[0])
-    gather_wait("slab", k, ns, cg, cg_ss, cg_rs)
+    gather_wait("slab", k, ns, cgw, cg_ss, cg_rs)
+    for i in range(ns):
+        cg[i, :count // 2] = cgw[i, :, :count]
+        cg[i, count // 2:] = cgw[i, :, count:]
     gather_wait("slab", k, ns, sbuf.at[0], s_ss.at[0], s_rs.at[0])
     rhs_first = [sbuf[0, i, 0:1] for i in range(ns)]
     share, square = chain(rhs_first)
+    slab_dot = jnp.sum(tile_sum(sbuf.at[0], ns)[1:2], axis=1, keepdims=True)
     sub_wide = lax.broadcasted_iota(jnp.int32, (8, nq * count), 0)
-    rbuf[0, q] = jnp.where(sub_wide == 0, share, square)
+    rbuf[0, q] = jnp.where(sub_wide == 0, share, square + slab_dot)
     gather_start("quad", q, nq, rbuf.at[0], r_ss.at[0], r_rs.at[0])
-    rz_block = jnp.sum(tile_sum(sbuf.at[0], ns)[1:2], axis=1, keepdims=True)
     gather_wait("quad", q, nq, rbuf.at[0], r_ss.at[0], r_rs.at[0])
     table, total = own_table(0)
-    rz = rz_block + total[1:2, 0:1]
+    rz = total[1:2, 0:1]
     for j in range(cz):
         p0[j] = bj[j] + interpolate(table, j)
     halo_start(1, p0)
@@ -297,51 +312,54 @@
 
     qbuf[1, q] = message(restrict(image), partial(direction, image))
     gather_start("quad", q, nq, qbuf.at[1], q_ss.at[1], q_rs.at[1])
-    image_block = solve_lines([q0[j] for j in range(cz)])
+    image = [q0[j] for j in range(cz)]
+    image_block = solve_lines(image)
     for j in range(cz):
         zz[j] = image_block[j]
+    cross, own_dot = partial(image, [bj[j] for j in range(cz)]), partial(image, image_block)
     gather_wait("quad", q, nq, qbuf.at[1], q_ss.at[1], q_rs.at[1])
-    sbuf[1, k] = message(coarse_rhs(1), tile_sum(qbuf.at[1], nq)[1:2])
+    sbuf[1, k] = jnp.where(sub8 < 2, message(coarse_rhs(1), tile_sum(qbuf.at[1], nq)[1:2]),
+                           jnp.where(sub8 == 2, cross, own_dot))
     gather_start("slab", k, ns, sbuf.at[1], s_ss.at[1], s_rs.at[1])
     gather_wait("slab", k, ns, sbuf.at[1], s_ss.at[1], s_rs.at[1])
-    alpha = rz / jnp.sum(tile_sum(sbuf.at[1], ns)[1:2], axis=1, keepdims=True)
+    sums = jnp.sum(tile_sum(sbuf.at[1], ns), axis=1, keepdims=True)
+    alpha = rz / sums[1:2]
     share, square = chain([sbuf[0, i, 0:1] - alpha * sbuf[1, i, 0:1] for i in range(ns)])
-    resid = [b_ref[j] - alpha * q0[j] for j in range(cz)]
-    block = [bj[j] - alpha * zz[j] for j in range(cz)]
-    for j in range(cz):
-        r_ref[j] = resid[j]
-        bj[j] = block[j]
-    dots = jnp.concatenate([partial(resid, block)] + [jnp.zeros((1, 128), F32)] * (nq * count // 128 - 1), axis=1)
-    rbuf[1, q] = jnp.where(sub_wide == 0, share, jnp.where(sub_wide == 1, square, dots))
+    square = square + slab_dot - 2.0 * alpha * sums[2:3] + alpha * alpha * sums[3:4]
+    rbuf[1, q] = jnp.where(sub_wide == 0, share, square)
     gather_start("quad", q, nq, rbuf.at[1], r_ss.at[1], r_rs.at[1])
+    for j in range(cz):
+        r_ref[j] = b_ref[j] - alpha * q0[j]
+        x_ref[j] = alpha * p0[j]
+        bj[j] = bj[j] - alpha * zz[j]
+    outs = [pltpu.make_async_copy(src, dst, out_sem.at[i]) for i, (src, dst) in enumerate((
+        (x_ref, x_out), (zz, p_out), (r_ref, r_out), (q0, q_out)))]
+    outs[0].start()
+    outs[2].start()
     gather_wait("quad", q, nq, rbuf.at[1], r_ss.at[1], r_rs.at[1])
     table, total = own_table(1)
-    dbuf[k] = jnp.broadcast_to(total[2:3, :128], (8, 128))
-    gather_start("slab", k, ns, dbuf, d_ss, d_rs)
-    for j in range(cz):
-        zz[j] = bj[j] + interpolate(table, j)
+    rz_next = total[1:2, 0:1]
+    beta = rz_next / rz
+    for j in range(cz):
+        zz[j] = bj[j] + interpolate(table, j) + beta * p0[j]
     halo_start(2, zz)
     halo_wait(2, zz)
-    image = apply(2, [zz[j] for j in range(cz)])
-    gather_wait("slab", k, ns, dbuf, d_ss, d_rs)
-    rz_next = total[1:2, 0:1] + jnp.sum(tile_sum(dbuf, ns)[0:1], axis=1, keepdims=True)
-    beta = rz_next / rz
-    direction = [zz[j] + beta * p0[j] for j in range(cz)]
-    image = [image[j] + beta * q0[j] for j in range(cz)]
+    direction = [zz[j] for j in range(cz)]
+    image = apply(2, direction)
     ebuf[q] = jnp.broadcast_to(partial(direction, image), (8, 128))
     gather_start("quad", q, nq, ebuf, e_ss, e_rs)
     for j in range(cz):
-        zz[j] = direction[j]
         q0[j] = image[j]
-        x_ref[j] = alpha * p0[j]
+    outs[1].start()
+    outs[3].start()
     gather_wait("quad", q, nq, ebuf, e_ss, e_rs)
     fbuf[k] = tile_sum(ebuf, nq)
     gather_start("slab", k, ns, fbuf, f_ss, f_rs)
     gather_wait("slab", k, ns, fbuf, f_ss, f_rs)
     last = rz_next / jnp.sum(tile_sum(fbuf, ns)[0:1], axis=1, keepdims=True)
-    for j in range(cz):
-        x_ref[j] = x_ref[j] + last * zz[j]
-        r_ref[j] = r_ref[j] - last * q0[j]
+    step_ref[...] = jnp.broadcast_to(last, (1, nx))
+    for c in outs:
+        c.wait()
     for c in pending:
         c.wait_send()
 
@@ -355,27 +373,33 @@
         field = pltpu.VMEM((cz, cy, nx), F32)
         dma = pltpu.SemaphoreType.DMA
         shape = jax.ShapeDtypeStruct((cz, cy, nx), F32)
-        return tuple(pl.pallas_call(
+        hbm = pl.BlockSpec(memory_space=pltpu.HBM)
+        x_part, p_part, r_part, q_part, step = pl.pallas_call(
             functools.partial(kernel, ns, nq),
-            out_shape=(shape, shape),
-            in_specs=[pl.BlockSpec(memory_space=pltpu.VMEM)] * 6,
-            out_specs=(pl.BlockSpec(memory_space=pltpu.VMEM),) * 2,
+            out_shape=(shape, shape, shape, shape, jax.ShapeDtypeStruct((1, nx), F32)),
+            in_specs=[hbm] * 6,
+            out_specs=(hbm,) * 4 + (pl.BlockSpec(memory_space=pltpu.VMEM),),
             scratch_shapes=[
+                field, pltpu.VMEM((cz, cy, nx), jnp.int32), field, pltpu.VMEM((cz, cy, nx), jnp.int32),
+                pltpu.VMEM(block_factor.shape, F32), pltpu.VMEM(coupling.shape, F32), field, field,
+                dma((6,)), dma((4,)),
                 pltpu.VMEM((cz + 1, cy, nx), F32), field, field, field, field, field, field, field,
                 pltpu.VMEM((cz, 8, cy, nx), BF16), pltpu.VMEM((cz, 8 * cy, nx), BF16),
                 field, field, field, field,
-                pltpu.VMEM((ns, count, count), F32),
+                pltpu.VMEM((ns, count, count), F32), pltpu.VMEM((ns, count // 2, 2 * count), F32),
                 pltpu.VMEM((2, nq, 8, 128), F32), pltpu.VMEM((2, ns, 8, 128), F32),
-                pltpu.VMEM((2, nq, 8, nq * count), F32), pltpu.VMEM((ns, 8, 128), F32),
+                pltpu.VMEM((2, nq, 8, nq * count), F32),
                 pltpu.VMEM((nq, 8, 128), F32), pltpu.VMEM((ns, 8, 128), F32),
                 pltpu.VMEM((3, 2, cy, nx), F32), pltpu.VMEM((3, 2, cz, nx), F32), pltpu.VMEM((3, 2, cz, nx), F32),
                 dma((ns,)), dma((ns,)), dma((2, nq)), dma((2, nq)), dma((2, ns)), dma((2, ns)),
-                dma((2, nq)), dma((2, nq)), dma((ns,)), dma((ns,)), dma((nq,)), dma((nq,)),
+                dma((2, nq)), dma((2, nq)), dma((nq,)), dma((nq,)),
                 dma((ns,)), dma((ns,)), dma((3, 4)), dma((3, 4)),
             ],
             compiler_params=pltpu.CompilerParams(
                 collective_id=0, has_side_effects=True, vmem_limit_bytes=40 * 1024 * 1024),
-        )(right_side, phase_label, density_gain, subdomain, block_factor, coupling))
+        )(*(pltpu.with_memory_space_constraint(value, pltpu.HBM) for value in (
+            right_side, phase_label, density_gain, subdomain, block_factor, coupling)))
+        return x_part + step * p_part, r_part - step * q_part
 
     spec = P("slab", "quad", None)
     return jax.shard_map(body, mesh=mesh, in_specs=(spec,) * 6, out_specs=(spec, spec), check_vma=False)

time: 60.3 us -> 49.8 us (0.83)
  local copies, waits for them, and re-layouts: 6.8 us -> 0 us
  Pallas kernels: 52.5 us -> 48.1 us
  other arithmetic: 0 us -> 0.87 us
    unnamed x14 -> x0, local copies, waits for them, and re-layouts: 6.8 us -> none
    pallas_call x1, Pallas kernels: 52.5 us -> 48.1 us  [body(): pl.pallas_call(functools.partial(kernel, ns, nq), out_shape=(shape, shape...]
    sub x0 -> x1, other arithmetic: none -> 0.87 us  [body(): return (x_part + step * p_part, r_part - step * q_part)]
where the time goes in v2:
time: 49.8 us; the launch traced here: 49.6 us
  Pallas kernels  48.1 us (97%)
  other arithmetic  0.87 us (2%)
  between operations  0.64 us (1%)
    pallas_call x1, Pallas kernels, body(): pl.pallas_call(functools.partial(kernel, ns, nq), out_shape=(shape, shape...  48.1 us

profile of v2, /device:TPU:0, one launch (start us, length us, event | category | flops | bytes accessed | tf_op | source)
XLA Modules:
  0.0 49.6 jit_solution(18315312641902077708)
XLA Ops:
  0.6 48.1 %shard_map.77 = (f32[4,16,1024]{2,1,0:T(8,128)S(1)}, f32[4,16,1024]{2,1,0:T(8,128)S(1)}, f32[4,16,1024]{2,1,0:T(8,128)S(1)}, f32[4,16,1024]{2,1,0:T(8,128)S(1)}, f32[1,1024]{1,0:T(1,128)S(1)}) custom-call(f32[4,16,1024]{2,1,0:T(8,128)} %b_hbm.1, s32[4,16,1024]{2,1,0:T(8,128)} %phase_hbm.1, f32[4,16,1024]{2,1,0:T(8,128)} %gain_hbm.1, s32[4,16,1024]{2,1,0:T(8,128)} %sub_hbm.1, ...), custom_call_target="tpu_custom_call" | custom-call | tf_op jit(solution)/shard_map/pallas_call | solution.py:377
  48.8 0.9 %multiply_subtract_fusion = (f32[4,16,1024]{2,1,0:T(8,128)}, f32[4,16,1024]{2,1,0:T(8,128)}) fusion(f32[4,16,1024]{2,1,0:T(8,128)S(1)} %get-tuple-element.10, f32[4,16,1024]{2,1,0:T(8,128)S(1)} %get-tuple-element.11, f32[1024]{0:T(1024)S(1)} %bitcast.1, f32[4,16,1024]{2,1,0:T(8,128)S(1)} %get-tuple-element.7, f32[4,16,1024]{2,1,0:T(8,128)S(1)} %get-tuple-element.9), kind=kLoop, calls=%fused_computation | loop fusion | flops 262144 | bytes 1576960 | tf_op jit(solution)/shard_map/sub | solution.py:402

commit v3 on v2

--- a/solution.py
+++ b/solution.py
@@ -17,6 +17,7 @@
 def kernel(ns, nq, b_hbm, phase_hbm, gain_hbm, sub_hbm, fac_hbm, cpl_hbm, x_out, p_out, r_out, q_out, step_ref,
            b_ref, phase_ref, gain_ref, sub_ref, fac_ref, cpl_ref, x_ref, r_ref, in_sem, out_sem, kz, kyl, kyh, kxl, kxh, diag, inv, gam, hot_hi, hot_lo, p0, q0, bj, zz,
            cg, cgw, qbuf, sbuf, rbuf, ebuf, fbuf, zhalo, yhalo, ysend,
+           fach, zsub, ysub, ysend_sub, zp, zq, yp,
            cg_ss, cg_rs, q_ss, q_rs, s_ss, s_rs, r_ss, r_rs, e_ss, e_rs, f_ss, f_rs, h_ss, h_rs):
     k = lax.axis_index("slab")
     q = lax.axis_index("quad")
@@ -62,6 +63,8 @@
     eye = (lax.broadcasted_iota(jnp.int32, (count, count), 0)
            == lax.broadcasted_iota(jnp.int32, (count, count), 1)).astype(F32)
 
+    halos = [(zhalo.at[i], yhalo.at[i], ysend.at[i]) for i in range(3)] + [(zsub, ysub, ysend_sub)]
+
     def halo_parts(slot, src):
         up, down = jnp.minimum(k + 1, ns - 1), jnp.maximum(k - 1, 0)
         right, left = jnp.minimum(q + 1, nq - 1), jnp.maximum(q - 1, 0)
@@ -71,24 +74,35 @@
                 src_ref=s, dst_ref=dst, send_sem=h_ss.at[slot, i], recv_sem=h_rs.at[slot, i],
                 device_id={axis: to}, device_id_type=MESH)
 
+        if slot == 4:
+            return ((k < ns - 1, k > 0, copy(src, fach.at[0], 0, "slab", up)),
+                    (k > 0, k < ns - 1, copy(src, fach.at[1], 1, "slab", down)))
+        zdst, ydst, ysrc = halos[slot]
         return (
-            (k < ns - 1, k > 0, copy(src.at[cz - 1], zhalo.at[slot, 0], 0, "slab", up)),
-            (k > 0, k < ns - 1, copy(src.at[0], zhalo.at[slot, 1], 1, "slab", down)),
-            (q < nq - 1, q > 0, copy(ysend.at[slot, 1], yhalo.at[slot, 0], 2, "quad", right)),
-            (q > 0, q < nq - 1, copy(ysend.at[slot, 0], yhalo.at[slot, 1], 3, "quad", left)),
+            (k < ns - 1, k > 0, copy(src.at[cz - 1], zdst.at[0], 0, "slab", up)),
+            (k > 0, k < ns - 1, copy(src.at[0], zdst.at[1], 1, "slab", down)),
+            (q < nq - 1, q > 0, copy(ysrc.at[1], ydst.at[0], 2, "quad", right)),
+            (q > 0, q < nq - 1, copy(ysrc.at[0], ydst.at[1], 3, "quad", left)),
         )
 
-    def halo_clear(slot):
-        for buf, i, edge in ((zhalo, 0, k == 0), (zhalo, 1, k == ns - 1),
-                             (yhalo, 0, q == 0), (yhalo, 1, q == nq - 1)):
+    def halo_clear():
+        for zdst, ydst, unused in halos:
+            for buf, i, edge in ((zdst, 0, k == 0), (zdst, 1, k == ns - 1),
+                                 (ydst, 0, q == 0), (ydst, 1, q == nq - 1)):
+                @pl.when(edge)
+                def _(buf=buf, i=i):
+                    buf[i] = jnp.zeros(buf.shape[1:], buf.dtype)
+        for i, edge in ((0, k == 0), (1, k == ns - 1)):
             @pl.when(edge)
-            def _(buf=buf, i=i):
-                buf[slot, i] = jnp.zeros(buf.shape[2:], F32)
+            def _(i=i):
+                fach[i] = jnp.zeros(fach.shape[1:], F32)
 
     def halo_start(slot, src):
-        for j in range(cz):
-            ysend[slot, 0, j:j + 1] = src[j, 0:1]
-            ysend[slot, 1, j:j + 1] = src[j, cy - 1:cy]
+        if slot < 4:
+            ysrc = halos[slot][2]
+            for j in range(cz):
+                ysrc[0, j:j + 1] = src[j, 0:1]
+                ysrc[1, j:j + 1] = src[j, cy - 1:cy]
         for sends, unused, c in halo_parts(slot, src):
             @pl.when(sends)
             def _(c=c):
@@ -104,11 +118,11 @@
             def _(c=c):
                 c.wait_send()
 
-    def y_below(slot, plane, j):
-        return jnp.where(row == 0, yhalo[slot, 0, j:j + 1], pltpu.roll(plane, 1, 0))
-
-    def y_above(slot, plane, j):
-        return jnp.where(row == cy - 1, yhalo[slot, 1, j:j + 1], pltpu.roll(plane, cy - 1, 0))
+    def y_below(plane, edge):
+        return jnp.where(row == 0, edge, pltpu.roll(plane, 1, 0))
+
+    def y_above(plane, edge):
+        return jnp.where(row == cy - 1, edge, pltpu.roll(plane, cy - 1, 0))
 
     def harmonic(here, there):
         return jnp.where(there > 0, 2.0 * here * there / (here + there), here)
@@ -173,35 +187,46 @@
                 sq_row = sq_row + now * now
             us.append(now)
         w = us[ns - 1]
-        own_row = jnp.zeros((1, count), F32)
-        own_col = jnp.where(k == ns - 1, w, 0.0)
+        near_row = [jnp.zeros((1, count), F32)] * 3
+        near_col = [jnp.where(k + d == ns - 1, w, 0.0) for d in (-1, 0, 1)]
         for i in range(ns - 1, 0, -1):
             if i % 2:
                 w = jnp.sum(cg[i] * w, axis=0, keepdims=True) + us[i - 1]
-                own_row = jnp.where(k == i - 1, w, own_row)
+                near_row = [jnp.where(k + d == i - 1, w, old) for d, old in zip((-1, 0, 1), near_row)]
             else:
                 w = jnp.sum(cg[i] * w, axis=1, keepdims=True) + us[i - 1]
-                own_col = jnp.where(k == i - 1, w, own_col)
-        own = own_col + jnp.sum(eye * own_row, axis=1, keepdims=True)
+                near_col = [jnp.where(k + d == i - 1, w, old) for d, old in zip((-1, 0, 1), near_col)]
+        near = [col + jnp.sum(eye * line, axis=1, keepdims=True) for col, line in zip(near_col, near_row)]
         square = jnp.sum(sq_row, axis=1, keepdims=True) + jnp.sum(sq_col, axis=0, keepdims=True)
-        share = jnp.sum(fac_ref[0] * own, axis=0, keepdims=True)
-        return share, square
-
-    def interpolate(table, j):
-        wide = jnp.broadcast_to(table, (cy, 128))
+        factors = (fach[0], fac_ref[0], fach[1])
+        shares = [jnp.sum(f * w, axis=0, keepdims=True) for f, w in zip(factors, near)]
+        return shares, square
+
+    def pack_shares(shares, scalar):
+        at = lax.broadcasted_iota(jnp.int32, (8, nq * count), 0)
+        return jnp.where(at == 0, shares[0], jnp.where(at == 1, shares[1], jnp.where(at == 2, shares[2], scalar)))
+
+    def gather_lanes(wide, index):
         return jnp.concatenate(
-            [jnp.take_along_axis(wide, sub_ref[j, :, 128 * c:128 * (c + 1)], axis=1, mode="promise_in_bounds")
+            [jnp.take_along_axis(wide, index[:, 128 * c:128 * (c + 1)], axis=1, mode="promise_in_bounds")
              for c in range(nx // 128)], axis=1)
 
-    def own_table(slot):
-        total = rbuf[slot, 0]
-        for i in range(1, nq):
-            total = total + rbuf[slot, i]
-        table = total[0:1, :128]
-        for i in range(1, nq // 2):
-            table = jnp.where(q // 2 == i, total[0:1, 128 * i:128 * (i + 1)], table)
-        table = jnp.where(q % 2 == 1, pltpu.roll(table, 64, 1), table)
-        return table, total
+    def interpolate(table, index):
+        return gather_lanes(jnp.broadcast_to(table, (cy, 128)), index)
+
+    def coarse_tables(slot):
+        total = tile_sum(rbuf.at[slot], nq)
+
+        def pick(at, quarter):
+            table = jnp.zeros((1, 128), F32)
+            for i in range(nq):
+                piece = total[at:at + 1, 128 * (i // 2):128 * (i // 2 + 1)]
+                table = jnp.where(quarter == i, pltpu.roll(piece, 64, 1) if i % 2 else piece, table)
+            return table
+
+        sides = jnp.concatenate(
+            [jnp.broadcast_to(pick(1, q - 1), (cz, 128)), jnp.broadcast_to(pick(1, q + 1), (cz, 128))], axis=0)
+        return pick(1, q), pick(0, q), pick(2, q), sides, total[3:4, 0:1]
 
     def tile_sum(buf, n):
         total = buf[0]
@@ -209,32 +234,19 @@
             total = total + buf[i]
         return total
 
-    def apply(slot, planes):
+    def apply(planes):
         images = []
         for j in range(cz):
-            below = planes[j - 1] if j > 0 else zhalo[slot, 0]
-            above = planes[j + 1] if j < cz - 1 else zhalo[slot, 1]
+            below = planes[j - 1] if j > 0 else zp[0]
+            above = planes[j + 1] if j < cz - 1 else zp[1]
             v = planes[j]
             images.append(
                 diag[j] * v - kz[j] * below - kz[j + 1] * above
-                - kyl[j] * y_below(slot, v, j) - kyh[j] * y_above(slot, v, j)
+                - kyl[j] * y_below(v, yp[j:j + 1]) - kyh[j] * y_above(v, yp[cz + j:cz + j + 1])
                 - kxl[j] * pltpu.roll(v, 1, 1) - kxh[j] * pltpu.roll(v, nx - 1, 1))
         return images
 
-    for slot in range(3):
-        halo_clear(slot)
-    loads[0].wait()
-    loads[1].wait()
-    for j in range(cz):
-        zz[j] = 1.0 / (gain_ref[j] * (0.001 + 0.999 * phase_ref[j].astype(F32)))
-    pl.semaphore_wait(barrier, ns - 1 + nq - 1)
-    halo_start(0, zz)
-    loads[2].wait()
-    couple = cpl_ref[0]
-    couple = jnp.where(k % 2 == 1, couple, couple.T)
-    cgw[k] = jnp.concatenate([couple[:count // 2], couple[count // 2:]], axis=1)
-    gather_start("slab", k, ns, cgw, cg_ss, cg_rs)
-
+    halo_clear()
     loads[3].wait()
     loads[4].wait()
     for j in range(cz):
@@ -245,10 +257,22 @@
         digit = lax.broadcasted_iota(jnp.int32, (8, nx), 0)
         hot_lo[j] = jnp.concatenate(
             [jnp.where(low[y:y + 1] == digit, 1.0, 0.0) for y in range(cy)], axis=0).astype(BF16)
-
     right_side = [b_ref[j] for j in range(cz)]
     qbuf[0, q] = jnp.broadcast_to(restrict(right_side), (8, 128))
+    pl.semaphore_wait(barrier, ns - 1 + nq - 1)
     gather_start("quad", q, nq, qbuf.at[0], q_ss.at[0], q_rs.at[0])
+    loads[0].wait()
+    loads[1].wait()
+    for j in range(cz):
+        zz[j] = 1.0 / (gain_ref[j] * (0.001 + 0.999 * phase_ref[j].astype(F32)))
+    halo_start(0, zz)
+    loads[2].wait()
+    couple = cpl_ref[0]
+    couple = jnp.where(k % 2 == 1, couple, couple.T)
+    cgw[k] = jnp.concatenate([couple[:count // 2], couple[count // 2:]], axis=1)
+    gather_start("slab", k, ns, cgw, cg_ss, cg_rs)
+    loads[5].wait()
+    halo_start(4, fac_ref.at[0])
 
     m = [zz[j] for j in range(cz)]
     kx_lo = []
@@ -258,13 +282,17 @@
         kx_lo.append(lo + hi)
         kxl[j] = jnp.where(lane == 0, 0.0, lo)
         kxh[j] = jnp.where(lane == nx - 1, 0.0, hi)
+    gather_wait("quad", q, nq, qbuf.at[0], q_ss.at[0], q_rs.at[0])
+    sbuf[0, k] = jnp.broadcast_to(coarse_rhs(0), (8, 128))
+    gather_start("slab", k, ns, sbuf.at[0], s_ss.at[0], s_rs.at[0])
+    halo_start(3, sub_ref)
     halo_wait(0, zz)
     kz[0] = harmonic(m[0], zhalo[0, 0])
     for j in range(1, cz):
         kz[j] = harmonic(m[j - 1], m[j])
     kz[cz] = harmonic(m[cz - 1], zhalo[0, 1])
     for j in range(cz):
-        lo = harmonic(m[j], y_below(0, m[j], j))
+        lo = harmonic(m[j], y_below(m[j], yhalo[0, 0, j:j + 1]))
         last = harmonic(m[j][cy - 1:cy], yhalo[0, 1, j:j + 1])
         hi = jnp.where(row == cy - 1, last, pltpu.roll(lo, cy - 1, 0))
         kyl[j] = lo
@@ -282,51 +310,55 @@
     block = solve_lines(right_side)
     for j in range(cz):
         bj[j] = block[j]
-    own_dot = partial(right_side, block)
-    loads[5].wait()
-    gather_wait("quad", q, nq, qbuf.at[0], q_ss.at[0], q_rs.at[0])
-    sbuf[0, k] = message(coarse_rhs(0), own_dot)
-    gather_start("slab", k, ns, sbuf.at[0], s_ss.at[0], s_rs.at[0])
+    halo_start(1, bj)
+    first_dot = partial(right_side, block)
     gather_wait("slab", k, ns, cgw, cg_ss, cg_rs)
     for i in range(ns):
         cg[i, :count // 2] = cgw[i, :, :count]
         cg[i, count // 2:] = cgw[i, :, count:]
+    halo_wait(4, fac_ref.at[0])
     gather_wait("slab", k, ns, sbuf.at[0], s_ss.at[0], s_rs.at[0])
     rhs_first = [sbuf[0, i, 0:1] for i in range(ns)]
-    share, square = chain(rhs_first)
-    slab_dot = jnp.sum(tile_sum(sbuf.at[0], ns)[1:2], axis=1, keepdims=True)
-    sub_wide = lax.broadcasted_iota(jnp.int32, (8, nq * count), 0)
-    rbuf[0, q] = jnp.where(sub_wide == 0, share, square + slab_dot)
+    shares, square = chain(rhs_first)
+    rbuf[0, q] = pack_shares(shares, square)
     gather_start("quad", q, nq, rbuf.at[0], r_ss.at[0], r_rs.at[0])
+    halo_wait(1, bj)
+    halo_wait(3, sub_ref)
+    ysub_all = jnp.concatenate([ysub[0], ysub[1]], axis=0)
     gather_wait("quad", q, nq, rbuf.at[0], r_ss.at[0], r_rs.at[0])
-    table, total = own_table(0)
-    rz = total[1:2, 0:1]
-    for j in range(cz):
-        p0[j] = bj[j] + interpolate(table, j)
-    halo_start(1, p0)
-    halo_wait(1, p0)
+    table, before, after, sides, first_square = coarse_tables(0)
+    for j in range(cz):
+        p0[j] = bj[j] + interpolate(table, sub_ref[j])
+    zp[0] = zhalo[1, 0] + interpolate(before, zsub[0])
+    zp[1] = zhalo[1, 1] + interpolate(after, zsub[1])
+    zq[0] = zp[0]
+    zq[1] = zp[1]
+    yp[...] = jnp.concatenate([yhalo[1, 0], yhalo[1, 1]], axis=0) + gather_lanes(sides, ysub_all)
     direction = [p0[j] for j in range(cz)]
-    image = apply(1, direction)
+    image = apply(direction)
     for j in range(cz):
         q0[j] = image[j]
 
-    qbuf[1, q] = message(restrict(image), partial(direction, image))
+    qbuf[1, q] = jnp.where(sub8 < 2, message(restrict(image), partial(direction, image)), first_dot)
     gather_start("quad", q, nq, qbuf.at[1], q_ss.at[1], q_rs.at[1])
     image = [q0[j] for j in range(cz)]
     image_block = solve_lines(image)
     for j in range(cz):
         zz[j] = image_block[j]
+    halo_start(2, zz)
     cross, own_dot = partial(image, [bj[j] for j in range(cz)]), partial(image, image_block)
     gather_wait("quad", q, nq, qbuf.at[1], q_ss.at[1], q_rs.at[1])
-    sbuf[1, k] = jnp.where(sub8 < 2, message(coarse_rhs(1), tile_sum(qbuf.at[1], nq)[1:2]),
-                           jnp.where(sub8 == 2, cross, own_dot))
+    quad_sum = tile_sum(qbuf.at[1], nq)
+    sbuf[1, k] = jnp.where(sub8 == 0, coarse_rhs(1), jnp.where(
+        sub8 == 1, quad_sum[1:2], jnp.where(sub8 == 2, quad_sum[2:3], jnp.where(sub8 == 3, cross, own_dot))))
     gather_start("slab", k, ns, sbuf.at[1], s_ss.at[1], s_rs.at[1])
     gather_wait("slab", k, ns, sbuf.at[1], s_ss.at[1], s_rs.at[1])
     sums = jnp.sum(tile_sum(sbuf.at[1], ns), axis=1, keepdims=True)
+    first_dot = sums[2:3]
+    rz = first_dot + first_square
     alpha = rz / sums[1:2]
-    share, square = chain([sbuf[0, i, 0:1] - alpha * sbuf[1, i, 0:1] for i in range(ns)])
-    square = square + slab_dot - 2.0 * alpha * sums[2:3] + alpha * alpha * sums[3:4]
-    rbuf[1, q] = jnp.where(sub_wide == 0, share, square)
+    shares, square = chain([sbuf[0, i, 0:1] - alpha * sbuf[1, i, 0:1] for i in range(ns)])
+    rbuf[1, q] = pack_shares(shares, square - 2.0 * alpha * sums[3:4] + alpha * alpha * sums[4:5])
     gather_start("quad", q, nq, rbuf.at[1], r_ss.at[1], r_rs.at[1])
     for j in range(cz):
         r_ref[j] = b_ref[j] - alpha * q0[j]
@@ -336,16 +368,21 @@
         (x_ref, x_out), (zz, p_out), (r_ref, r_out), (q0, q_out)))]
     outs[0].start()
     outs[2].start()
+    halo_wait(2, zz)
+    for i in range(2):
+        zp[i] = zhalo[1, i] - alpha * zhalo[2, i]
+    yedge = [yhalo[1, i] - alpha * yhalo[2, i] for i in range(2)]
     gather_wait("quad", q, nq, rbuf.at[1], r_ss.at[1], r_rs.at[1])
-    table, total = own_table(1)
-    rz_next = total[1:2, 0:1]
+    table, before, after, sides, last_square = coarse_tables(1)
+    rz_next = first_dot + last_square
     beta = rz_next / rz
     for j in range(cz):
-        zz[j] = bj[j] + interpolate(table, j) + beta * p0[j]
-    halo_start(2, zz)
-    halo_wait(2, zz)
+        zz[j] = bj[j] + interpolate(table, sub_ref[j]) + beta * p0[j]
+    zp[0] = zp[0] + interpolate(before, zsub[0]) + beta * zq[0]
+    zp[1] = zp[1] + interpolate(after, zsub[1]) + beta * zq[1]
+    yp[...] = jnp.concatenate(yedge, axis=0) + gather_lanes(sides, ysub_all) + beta * yp[...]
     direction = [zz[j] for j in range(cz)]
-    image = apply(2, direction)
+    image = apply(direction)
     ebuf[q] = jnp.broadcast_to(partial(direction, image), (8, 128))
     gather_start("quad", q, nq, ebuf, e_ss, e_rs)
     for j in range(cz):
@@ -391,9 +428,12 @@
                 pltpu.VMEM((2, nq, 8, nq * count), F32),
                 pltpu.VMEM((nq, 8, 128), F32), pltpu.VMEM((ns, 8, 128), F32),
                 pltpu.VMEM((3, 2, cy, nx), F32), pltpu.VMEM((3, 2, cz, nx), F32), pltpu.VMEM((3, 2, cz, nx), F32),
+                pltpu.VMEM((2,) + block_factor.shape[1:], F32), pltpu.VMEM((2, cy, nx), jnp.int32),
+                pltpu.VMEM((2, cz, nx), jnp.int32), pltpu.VMEM((2, cz, nx), jnp.int32),
+                pltpu.VMEM((2, cy, nx), F32), pltpu.VMEM((2, cy, nx), F32), pltpu.VMEM((2 * cz, nx), F32),
                 dma((ns,)), dma((ns,)), dma((2, nq)), dma((2, nq)), dma((2, ns)), dma((2, ns)),
                 dma((2, nq)), dma((2, nq)), dma((nq,)), dma((nq,)),
-                dma((ns,)), dma((ns,)), dma((3, 4)), dma((3, 4)),
+                dma((ns,)), dma((ns,)), dma((5, 4)), dma((5, 4)),
             ],
             compiler_params=pltpu.CompilerParams(
                 collective_id=0, has_side_effects=True, vmem_limit_bytes=40 * 1024 * 1024),

time: 49.8 us -> 43.4 us (0.87)
  Pallas kernels: 48.1 us -> 41.8 us
    pallas_call x1, Pallas kernels: 48.1 us -> 41.8 us  [body(): pl.pallas_call(functools.partial(kernel, ns, nq), out_shape=(shape, shape...]
where the time goes in v3:
time: 43.4 us; the launch traced here: 43.3 us
  Pallas kernels  41.8 us (96%)
  other arithmetic  0.87 us (2%)
  between operations  0.64 us (1%)
    pallas_call x1, Pallas kernels, body(): pl.pallas_call(functools.partial(kernel, ns, nq), out_shape=(shape, shape...  41.8 us

profile of v3, /device:TPU:0, one launch (start us, length us, event | category | flops | bytes accessed | tf_op | source)
XLA Modules:
  0.0 43.3 jit_solution(5471063579273226947)
XLA Ops:
  0.6 41.8 %shard_map.77 = (f32[4,16,1024]{2,1,0:T(8,128)S(1)}, f32[4,16,1024]{2,1,0:T(8,128)S(1)}, f32[4,16,1024]{2,1,0:T(8,128)S(1)}, f32[4,16,1024]{2,1,0:T(8,128)S(1)}, f32[1,1024]{1,0:T(1,128)S(1)}) custom-call(f32[4,16,1024]{2,1,0:T(8,128)} %b_hbm.1, s32[4,16,1024]{2,1,0:T(8,128)} %phase_hbm.1, f32[4,16,1024]{2,1,0:T(8,128)} %gain_hbm.1, s32[4,16,1024]{2,1,0:T(8,128)} %sub_hbm.1, ...), custom_call_target="tpu_custom_call" | custom-call | tf_op jit(solution)/shard_map/pallas_call | solution.py:414
  42.4 0.9 %multiply_subtract_fusion = (f32[4,16,1024]{2,1,0:T(8,128)}, f32[4,16,1024]{2,1,0:T(8,128)}) fusion(f32[4,16,1024]{2,1,0:T(8,128)S(1)} %get-tuple-element.10, f32[4,16,1024]{2,1,0:T(8,128)S(1)} %get-tuple-element.11, f32[1024]{0:T(1024)S(1)} %bitcast.1, f32[4,16,1024]{2,1,0:T(8,128)S(1)} %get-tuple-element.7, f32[4,16,1024]{2,1,0:T(8,128)S(1)} %get-tuple-element.9), kind=kLoop, calls=%fused_computation | loop fusion | flops 262144 | bytes 1576960 | tf_op jit(solution)/shard_map/sub | solution.py:442

commit v4 on v3

--- a/solution.py
+++ b/solution.py
@@ -59,6 +59,7 @@
     row = lax.broadcasted_iota(jnp.int32, (cy, nx), 0)
     lane = lax.broadcasted_iota(jnp.int32, (cy, nx), 1)
     sub8 = lax.broadcasted_iota(jnp.int32, (8, 128), 0)
+    lane1 = lax.broadcasted_iota(jnp.int32, (1, 128), 1)
     lane8 = lax.broadcasted_iota(jnp.int32, (8, 128), 1)
     eye = (lax.broadcasted_iota(jnp.int32, (count, count), 0)
            == lax.broadcasted_iota(jnp.int32, (count, count), 1)).astype(F32)
@@ -165,11 +166,16 @@
             values[j] = rho[j] - gam[j] * values[j + 1]
         return values
 
-    def message(first, second):
-        return jnp.where(sub8 == 0, first, second)
+    def pack(vector, *scalars):
+        for i, scalar in enumerate(scalars):
+            vector = jnp.where(lane1 == count + i, scalar, vector)
+        return vector
+
+    def dot(left, right):
+        return jnp.sum(partial(left, right), axis=1, keepdims=True)
 
     def coarse_rhs(slot):
-        rows = [qbuf[slot, i, 0:1] for i in range(nq)]
+        rows = [jnp.where(lane1 < count, qbuf[slot, i], 0.0) for i in range(nq)]
         pieces = [rows[2 * i] + pltpu.roll(rows[2 * i + 1], 64, 1) for i in range(nq // 2)]
         whole = jnp.concatenate(pieces, axis=1)
         column = jnp.sum(fac_ref[0] * whole, axis=1, keepdims=True)
@@ -203,8 +209,7 @@
         return shares, square
 
     def pack_shares(shares, scalar):
-        at = lax.broadcasted_iota(jnp.int32, (8, nq * count), 0)
-        return jnp.where(at == 0, shares[0], jnp.where(at == 1, shares[1], jnp.where(at == 2, shares[2], scalar)))
+        return jnp.concatenate(shares + [jnp.broadcast_to(scalar, (1, 128))], axis=1)
 
     def gather_lanes(wide, index):
         return jnp.concatenate(
@@ -220,13 +225,14 @@
         def pick(at, quarter):
             table = jnp.zeros((1, 128), F32)
             for i in range(nq):
-                piece = total[at:at + 1, 128 * (i // 2):128 * (i // 2 + 1)]
+                start = nq * count * at + 128 * (i // 2)
+                piece = total[:, start:start + 128]
                 table = jnp.where(quarter == i, pltpu.roll(piece, 64, 1) if i % 2 else piece, table)
             return table
 
         sides = jnp.concatenate(
             [jnp.broadcast_to(pick(1, q - 1), (cz, 128)), jnp.broadcast_to(pick(1, q + 1), (cz, 128))], axis=0)
-        return pick(1, q), pick(0, q), pick(2, q), sides, total[3:4, 0:1]
+        return pick(1, q), pick(0, q), pick(2, q), sides, total[:, 3 * nq * count:3 * nq * count + 1]
 
     def tile_sum(buf, n):
         total = buf[0]
@@ -258,7 +264,7 @@
         hot_lo[j] = jnp.concatenate(
             [jnp.where(low[y:y + 1] == digit, 1.0, 0.0) for y in range(cy)], axis=0).astype(BF16)
     right_side = [b_ref[j] for j in range(cz)]
-    qbuf[0, q] = jnp.broadcast_to(restrict(right_side), (8, 128))
+    qbuf[0, q] = restrict(right_side)
     pl.semaphore_wait(barrier, ns - 1 + nq - 1)
     gather_start("quad", q, nq, qbuf.at[0], q_ss.at[0], q_rs.at[0])
     loads[0].wait()
@@ -271,8 +277,6 @@
     couple = jnp.where(k % 2 == 1, couple, couple.T)
     cgw[k] = jnp.concatenate([couple[:count // 2], couple[count // 2:]], axis=1)
     gather_start("slab", k, ns, cgw, cg_ss, cg_rs)
-    loads[5].wait()
-    halo_start(4, fac_ref.at[0])
 
     m = [zz[j] for j in range(cz)]
     kx_lo = []
@@ -282,9 +286,11 @@
         kx_lo.append(lo + hi)
         kxl[j] = jnp.where(lane == 0, 0.0, lo)
         kxh[j] = jnp.where(lane == nx - 1, 0.0, hi)
+    loads[5].wait()
     gather_wait("quad", q, nq, qbuf.at[0], q_ss.at[0], q_rs.at[0])
-    sbuf[0, k] = jnp.broadcast_to(coarse_rhs(0), (8, 128))
+    sbuf[0, k] = coarse_rhs(0)
     gather_start("slab", k, ns, sbuf.at[0], s_ss.at[0], s_rs.at[0])
+    halo_start(4, fac_ref.at[0])
     halo_start(3, sub_ref)
     halo_wait(0, zz)
     kz[0] = harmonic(m[0], zhalo[0, 0])
@@ -311,14 +317,14 @@
     for j in range(cz):
         bj[j] = block[j]
     halo_start(1, bj)
-    first_dot = partial(right_side, block)
+    first_dot = dot(right_side, block)
     gather_wait("slab", k, ns, cgw, cg_ss, cg_rs)
     for i in range(ns):
         cg[i, :count // 2] = cgw[i, :, :count]
         cg[i, count // 2:] = cgw[i, :, count:]
     halo_wait(4, fac_ref.at[0])
     gather_wait("slab", k, ns, sbuf.at[0], s_ss.at[0], s_rs.at[0])
-    rhs_first = [sbuf[0, i, 0:1] for i in range(ns)]
+    rhs_first = [sbuf[0, i] for i in range(ns)]
     shares, square = chain(rhs_first)
     rbuf[0, q] = pack_shares(shares, square)
     gather_start("quad", q, nq, rbuf.at[0], r_ss.at[0], r_rs.at[0])
@@ -339,26 +345,26 @@
     for j in range(cz):
         q0[j] = image[j]
 
-    qbuf[1, q] = jnp.where(sub8 < 2, message(restrict(image), partial(direction, image)), first_dot)
+    qbuf[1, q] = pack(restrict(image), dot(direction, image), first_dot)
     gather_start("quad", q, nq, qbuf.at[1], q_ss.at[1], q_rs.at[1])
     image = [q0[j] for j in range(cz)]
     image_block = solve_lines(image)
     for j in range(cz):
         zz[j] = image_block[j]
     halo_start(2, zz)
-    cross, own_dot = partial(image, [bj[j] for j in range(cz)]), partial(image, image_block)
+    cross, own_dot = dot(image, [bj[j] for j in range(cz)]), dot(image, image_block)
     gather_wait("quad", q, nq, qbuf.at[1], q_ss.at[1], q_rs.at[1])
     quad_sum = tile_sum(qbuf.at[1], nq)
-    sbuf[1, k] = jnp.where(sub8 == 0, coarse_rhs(1), jnp.where(
-        sub8 == 1, quad_sum[1:2], jnp.where(sub8 == 2, quad_sum[2:3], jnp.where(sub8 == 3, cross, own_dot))))
+    sbuf[1, k] = pack(coarse_rhs(1), quad_sum[:, count:count + 1], quad_sum[:, count + 1:count + 2], cross, own_dot)
     gather_start("slab", k, ns, sbuf.at[1], s_ss.at[1], s_rs.at[1])
     gather_wait("slab", k, ns, sbuf.at[1], s_ss.at[1], s_rs.at[1])
-    sums = jnp.sum(tile_sum(sbuf.at[1], ns), axis=1, keepdims=True)
-    first_dot = sums[2:3]
+    total = tile_sum(sbuf.at[1], ns)
+    sums = [total[:, count + i:count + i + 1] for i in range(4)]
+    first_dot = sums[1]
     rz = first_dot + first_square
-    alpha = rz / sums[1:2]
-    shares, square = chain([sbuf[0, i, 0:1] - alpha * sbuf[1, i, 0:1] for i in range(ns)])
-    rbuf[1, q] = pack_shares(shares, square - 2.0 * alpha * sums[3:4] + alpha * alpha * sums[4:5])
+    alpha = rz / sums[0]
+    shares, square = chain([sbuf[0, i] - alpha * sbuf[1, i] for i in range(ns)])
+    rbuf[1, q] = pack_shares(shares, square - 2.0 * alpha * sums[2] + alpha * alpha * sums[3])
     gather_start("quad", q, nq, rbuf.at[1], r_ss.at[1], r_rs.at[1])
     for j in range(cz):
         r_ref[j] = b_ref[j] - alpha * q0[j]
@@ -383,7 +389,7 @@
     yp[...] = jnp.concatenate(yedge, axis=0) + gather_lanes(sides, ysub_all) + beta * yp[...]
     direction = [zz[j] for j in range(cz)]
     image = apply(direction)
-    ebuf[q] = jnp.broadcast_to(partial(direction, image), (8, 128))
+    ebuf[q] = partial(direction, image)
     gather_start("quad", q, nq, ebuf, e_ss, e_rs)
     for j in range(cz):
         q0[j] = image[j]
@@ -393,7 +399,7 @@
     fbuf[k] = tile_sum(ebuf, nq)
     gather_start("slab", k, ns, fbuf, f_ss, f_rs)
     gather_wait("slab", k, ns, fbuf, f_ss, f_rs)
-    last = rz_next / jnp.sum(tile_sum(fbuf, ns)[0:1], axis=1, keepdims=True)
+    last = rz_next / jnp.sum(tile_sum(fbuf, ns), axis=1, keepdims=True)
     step_ref[...] = jnp.broadcast_to(last, (1, nx))
     for c in outs:
         c.wait()
@@ -424,9 +430,9 @@
                 pltpu.VMEM((cz, 8, cy, nx), BF16), pltpu.VMEM((cz, 8 * cy, nx), BF16),
                 field, field, field, field,
                 pltpu.VMEM((ns, count, count), F32), pltpu.VMEM((ns, count // 2, 2 * count), F32),
-                pltpu.VMEM((2, nq, 8, 128), F32), pltpu.VMEM((2, ns, 8, 128), F32),
-                pltpu.VMEM((2, nq, 8, nq * count), F32),
-                pltpu.VMEM((nq, 8, 128), F32), pltpu.VMEM((ns, 8, 128), F32),
+                pltpu.VMEM((2, nq, 1, 128), F32), pltpu.VMEM((2, ns, 1, 128), F32),
+                pltpu.VMEM((2, nq, 1, 3 * nq * count + 128), F32),
+                pltpu.VMEM((nq, 1, 128), F32), pltpu.VMEM((ns, 1, 128), F32),
                 pltpu.VMEM((3, 2, cy, nx), F32), pltpu.VMEM((3, 2, cz, nx), F32), pltpu.VMEM((3, 2, cz, nx), F32),
                 pltpu.VMEM((2,) + block_factor.shape[1:], F32), pltpu.VMEM((2, cy, nx), jnp.int32),
                 pltpu.VMEM((2, cz, nx), jnp.int32), pltpu.VMEM((2, cz, nx), jnp.int32),

time: 43.4 us -> 42.7 us (0.984)
  Pallas kernels: 41.8 us -> 41.1 us
    pallas_call x1, Pallas kernels: 41.8 us -> 41.1 us  [body(): pl.pallas_call(functools.partial(kernel, ns, nq), out_shape=(shape, shape...]
where the time goes in v4:
time: 42.7 us; the launch traced here: 42.6 us
  Pallas kernels  41.1 us (96%)
  other arithmetic  0.87 us (2%)
  between operations  0.64 us (1%)
    pallas_call x1, Pallas kernels, body(): pl.pallas_call(functools.partial(kernel, ns, nq), out_shape=(shape, shape...  41.1 us
    sub x1, other arithmetic, body(): return (x_part + step * p_part, r_part - step * q_part)  0.87 us

profile of v4, /device:TPU:0, one launch (start us, length us, event | category | flops | bytes accessed | tf_op | source)
XLA Modules:
  0.0 42.6 jit_solution(10526609734126130412)
XLA Ops:
  0.6 41.1 %shard_map.77 = (f32[4,16,1024]{2,1,0:T(8,128)S(1)}, f32[4,16,1024]{2,1,0:T(8,128)S(1)}, f32[4,16,1024]{2,1,0:T(8,128)S(1)}, f32[4,16,1024]{2,1,0:T(8,128)S(1)}, f32[1,1024]{1,0:T(1,128)S(1)}) custom-call(f32[4,16,1024]{2,1,0:T(8,128)} %b_hbm.1, s32[4,16,1024]{2,1,0:T(8,128)} %phase_hbm.1, f32[4,16,1024]{2,1,0:T(8,128)} %gain_hbm.1, s32[4,16,1024]{2,1,0:T(8,128)} %sub_hbm.1, ...), custom_call_target="tpu_custom_call" | custom-call | tf_op jit(solution)/shard_map/pallas_call | solution.py:420
  41.7 0.9 %multiply_subtract_fusion = (f32[4,16,1024]{2,1,0:T(8,128)}, f32[4,16,1024]{2,1,0:T(8,128)}) fusion(f32[4,16,1024]{2,1,0:T(8,128)S(1)} %get-tuple-element.10, f32[4,16,1024]{2,1,0:T(8,128)S(1)} %get-tuple-element.11, f32[1024]{0:T(1024)S(1)} %bitcast.1, f32[4,16,1024]{2,1,0:T(8,128)S(1)} %get-tuple-element.7, f32[4,16,1024]{2,1,0:T(8,128)S(1)} %get-tuple-element.9), kind=kLoop, calls=%fused_computation | loop fusion | flops 262144 | bytes 1576960 | tf_op jit(solution)/shard_map/sub | solution.py:448

commit v5 on v4

--- a/solution.py
+++ b/solution.py
@@ -253,7 +253,19 @@
         return images
 
     halo_clear()
+    loads[0].wait()
+    loads[1].wait()
+    for j in range(cz):
+        zz[j] = 1.0 / (gain_ref[j] * (0.001 + 0.999 * phase_ref[j].astype(F32)))
     loads[3].wait()
+    pl.semaphore_wait(barrier, ns - 1 + nq - 1)
+    halo_start(0, zz)
+    loads[2].wait()
+    couple = cpl_ref[0]
+    couple = jnp.where(k % 2 == 1, couple, couple.T)
+    cgw[k] = jnp.concatenate([couple[:count // 2], couple[count // 2:]], axis=1)
+    gather_start("slab", k, ns, cgw, cg_ss, cg_rs)
+    halo_start(3, sub_ref)
     loads[4].wait()
     for j in range(cz):
         label = sub_ref[j]
@@ -265,18 +277,7 @@
             [jnp.where(low[y:y + 1] == digit, 1.0, 0.0) for y in range(cy)], axis=0).astype(BF16)
     right_side = [b_ref[j] for j in range(cz)]
     qbuf[0, q] = restrict(right_side)
-    pl.semaphore_wait(barrier, ns - 1 + nq - 1)
     gather_start("quad", q, nq, qbuf.at[0], q_ss.at[0], q_rs.at[0])
-    loads[0].wait()
-    loads[1].wait()
-    for j in range(cz):
-        zz[j] = 1.0 / (gain_ref[j] * (0.001 + 0.999 * phase_ref[j].astype(F32)))
-    halo_start(0, zz)
-    loads[2].wait()
-    couple = cpl_ref[0]
-    couple = jnp.where(k % 2 == 1, couple, couple.T)
-    cgw[k] = jnp.concatenate([couple[:count // 2], couple[count // 2:]], axis=1)
-    gather_start("slab", k, ns, cgw, cg_ss, cg_rs)
 
     m = [zz[j] for j in range(cz)]
     kx_lo = []
@@ -291,7 +292,6 @@
     sbuf[0, k] = coarse_rhs(0)
     gather_start("slab", k, ns, sbuf.at[0], s_ss.at[0], s_rs.at[0])
     halo_start(4, fac_ref.at[0])
-    halo_start(3, sub_ref)
     halo_wait(0, zz)
     kz[0] = harmonic(m[0], zhalo[0, 0])
     for j in range(1, cz):

time: 42.7 us -> 44.3 us (1.037)
  Pallas kernels: 41.1 us -> 42.7 us
    pallas_call x1, Pallas kernels: 41.1 us -> 42.7 us  [body(): pl.pallas_call(functools.partial(kernel, ns, nq), out_shape=(shape, shape...]
where the time goes in v5:
time: 44.3 us; the launch traced here: 44.2 us
  Pallas kernels  42.7 us (96%)
  other arithmetic  0.87 us (2%)
  between operations  0.64 us (1%)
    pallas_call x1, Pallas kernels, body(): pl.pallas_call(functools.partial(kernel, ns, nq), out_shape=(shape, shape...  42.7 us

profile of v5, /device:TPU:0, one launch (start us, length us, event | category | flops | bytes accessed | tf_op | source)
XLA Modules:
  0.0 44.2 jit_solution(2589267901090995146)
XLA Ops:
  0.6 42.7 %shard_map.77 = (f32[4,16,1024]{2,1,0:T(8,128)S(1)}, f32[4,16,1024]{2,1,0:T(8,128)S(1)}, f32[4,16,1024]{2,1,0:T(8,128)S(1)}, f32[4,16,1024]{2,1,0:T(8,128)S(1)}, f32[1,1024]{1,0:T(1,128)S(1)}) custom-call(f32[4,16,1024]{2,1,0:T(8,128)} %b_hbm.1, s32[4,16,1024]{2,1,0:T(8,128)} %phase_hbm.1, f32[4,16,1024]{2,1,0:T(8,128)} %gain_hbm.1, s32[4,16,1024]{2,1,0:T(8,128)} %sub_hbm.1, ...), custom_call_target="tpu_custom_call" | custom-call | tf_op jit(solution)/shard_map/pallas_call | solution.py:420
  43.3 0.9 %multiply_subtract_fusion = (f32[4,16,1024]{2,1,0:T(8,128)}, f32[4,16,1024]{2,1,0:T(8,128)}) fusion(f32[4,16,1024]{2,1,0:T(8,128)S(1)} %get-tuple-element.10, f32[4,16,1024]{2,1,0:T(8,128)S(1)} %get-tuple-element.11, f32[1024]{0:T(1024)S(1)} %bitcast.1, f32[4,16,1024]{2,1,0:T(8,128)S(1)} %get-tuple-element.7, f32[4,16,1024]{2,1,0:T(8,128)S(1)} %get-tuple-element.9), kind=kLoop, calls=%fused_computation | loop fusion | flops 262144 | bytes 1576960 | tf_op jit(solution)/shard_map/sub | solution.py:448

commit v6 on v4

--- a/solution.py
+++ b/solution.py
@@ -25,8 +25,8 @@
     count = cpl_ref.shape[2]
     pending = []
     loads = [pltpu.make_async_copy(src, dst, in_sem.at[i]) for i, (src, dst) in enumerate((
-        (phase_hbm, phase_ref), (gain_hbm, gain_ref), (cpl_hbm, cpl_ref),
-        (sub_hbm, sub_ref), (b_hbm, b_ref), (fac_hbm, fac_ref)))]
+        (sub_hbm, sub_ref), (b_hbm, b_ref), (phase_hbm, phase_ref),
+        (gain_hbm, gain_ref), (cpl_hbm, cpl_ref), (fac_hbm, fac_ref)))]
     for c in loads:
         c.start()
 
@@ -253,8 +253,8 @@
         return images
 
     halo_clear()
-    loads[3].wait()
-    loads[4].wait()
+    loads[0].wait()
+    loads[1].wait()
     for j in range(cz):
         label = sub_ref[j]
         high, low = label >> 3, label & 7
@@ -267,31 +267,31 @@
     qbuf[0, q] = restrict(right_side)
     pl.semaphore_wait(barrier, ns - 1 + nq - 1)
     gather_start("quad", q, nq, qbuf.at[0], q_ss.at[0], q_rs.at[0])
-    loads[0].wait()
-    loads[1].wait()
+    loads[2].wait()
+    loads[3].wait()
     for j in range(cz):
         zz[j] = 1.0 / (gain_ref[j] * (0.001 + 0.999 * phase_ref[j].astype(F32)))
     halo_start(0, zz)
-    loads[2].wait()
+    loads[4].wait()
     couple = cpl_ref[0]
     couple = jnp.where(k % 2 == 1, couple, couple.T)
     cgw[k] = jnp.concatenate([couple[:count // 2], couple[count // 2:]], axis=1)
     gather_start("slab", k, ns, cgw, cg_ss, cg_rs)
 
-    m = [zz[j] for j in range(cz)]
-    kx_lo = []
-    for j in range(cz):
-        lo = jnp.where(lane == 0, m[j], harmonic(m[j], pltpu.roll(m[j], 1, 1)))
-        hi = jnp.where(lane == nx - 1, m[j], pltpu.roll(lo, nx - 1, 1))
-        kx_lo.append(lo + hi)
-        kxl[j] = jnp.where(lane == 0, 0.0, lo)
-        kxh[j] = jnp.where(lane == nx - 1, 0.0, hi)
     loads[5].wait()
     gather_wait("quad", q, nq, qbuf.at[0], q_ss.at[0], q_rs.at[0])
     sbuf[0, k] = coarse_rhs(0)
     gather_start("slab", k, ns, sbuf.at[0], s_ss.at[0], s_rs.at[0])
     halo_start(4, fac_ref.at[0])
     halo_start(3, sub_ref)
+    m = [zz[j] for j in range(cz)]
+    kx_lo = []
+    for j in range(cz):
+        lo = jnp.where(lane == 0, m[j], harmonic(m[j], pltpu.roll(m[j], 1, 1)))
+        hi = jnp.where(lane == nx - 1, m[j], pltpu.roll(lo, nx - 1, 1))
+        kx_lo.append(lo + hi)
+        kxl[j] = jnp.where(lane == 0, 0.0, lo)
+        kxh[j] = jnp.where(lane == nx - 1, 0.0, hi)
     halo_wait(0, zz)
     kz[0] = harmonic(m[0], zhalo[0, 0])
     for j in range(1, cz):
@@ -398,13 +398,13 @@
     gather_wait("quad", q, nq, ebuf, e_ss, e_rs)
     fbuf[k] = tile_sum(ebuf, nq)
     gather_start("slab", k, ns, fbuf, f_ss, f_rs)
-    gather_wait("slab", k, ns, fbuf, f_ss, f_rs)
-    last = rz_next / jnp.sum(tile_sum(fbuf, ns), axis=1, keepdims=True)
-    step_ref[...] = jnp.broadcast_to(last, (1, nx))
     for c in outs:
         c.wait()
     for c in pending:
         c.wait_send()
+    gather_wait("slab", k, ns, fbuf, f_ss, f_rs)
+    last = rz_next / jnp.sum(tile_sum(fbuf, ns), axis=1, keepdims=True)
+    step_ref[...] = jnp.broadcast_to(last, (1, nx))
 
 
 def solution(mesh):

time: 42.7 us -> 42.8 us (level)
  no operation moved by 1% of the time
where the time goes in v6:
time: 42.8 us; the launch traced here: 42.7 us
  Pallas kernels  41.2 us (96%)
  other arithmetic  0.87 us (2%)
  between operations  0.64 us (1%)
    pallas_call x1, Pallas kernels, body(): pl.pallas_call(functools.partial(kernel, ns, nq), out_shape=(shape, shape...  41.2 us
    sub x1, other arithmetic, body(): return (x_part + step * p_part, r_part - step * q_part)  0.87 us

profile of v6, /device:TPU:0, one launch (start us, length us, event | category | flops | bytes accessed | tf_op | source)
XLA Modules:
  0.0 42.7 jit_solution(14274351551757188708)
XLA Ops:
  0.6 41.2 %shard_map.77 = (f32[4,16,1024]{2,1,0:T(8,128)S(1)}, f32[4,16,1024]{2,1,0:T(8,128)S(1)}, f32[4,16,1024]{2,1,0:T(8,128)S(1)}, f32[4,16,1024]{2,1,0:T(8,128)S(1)}, f32[1,1024]{1,0:T(1,128)S(1)}) custom-call(f32[4,16,1024]{2,1,0:T(8,128)} %b_hbm.1, s32[4,16,1024]{2,1,0:T(8,128)} %phase_hbm.1, f32[4,16,1024]{2,1,0:T(8,128)} %gain_hbm.1, s32[4,16,1024]{2,1,0:T(8,128)} %sub_hbm.1, ...), custom_call_target="tpu_custom_call" | custom-call | tf_op jit(solution)/shard_map/pallas_call | solution.py:420
  41.8 0.9 %multiply_subtract_fusion = (f32[4,16,1024]{2,1,0:T(8,128)}, f32[4,16,1024]{2,1,0:T(8,128)}) fusion(f32[4,16,1024]{2,1,0:T(8,128)S(1)} %get-tuple-element.10, f32[4,16,1024]{2,1,0:T(8,128)S(1)} %get-tuple-element.11, f32[1024]{0:T(1024)S(1)} %bitcast.1, f32[4,16,1024]{2,1,0:T(8,128)S(1)} %get-tuple-element.7, f32[4,16,1024]{2,1,0:T(8,128)S(1)} %get-tuple-element.9), kind=kLoop, calls=%fused_computation | loop fusion | flops 262144 | bytes 1576960 | tf_op jit(solution)/shard_map/sub | solution.py:448
